TPU v7x, 512 devices: a whole 4x4x16 slice. The times are simulated.
512 devices in a mesh: ctx: 64 (over z, x), tp: 8 (over y, core).
Axes of the slice: x: 4, y: 4, z: 16, core: 2. Of those that a mesh axis runs over, the one named last changes fastest.
Arguments:
- queries: bfloat16 [16384, 16384], P('ctx', 'tp'), may hold values from -4 to 4
- keys: bfloat16 [16384, 1024], P('ctx', 'tp'), may hold values from -4 to 4
- values: bfloat16 [16384, 1024], P('ctx', 'tp'), may hold values from -4 to 4
- attn_out: bfloat16 [16384, 16384], P('ctx', 'tp'), may hold values from -4 to 4
- grad_out: bfloat16 [16384, 16384], P('ctx', 'tp'), may hold values from -8 to 8
- log_norm: float32 [128, 16384], P('tp', 'ctx'), may hold values from 0 to 4
- doc_start: int32 [16384], P('ctx'), may hold values from 0 to 16383, as said below
Outputs:
- grad_queries: bfloat16 [16384, 16384], P('ctx', 'tp')
- grad_keys: bfloat16 [16384, 1024], P('ctx', 'tp')
- grad_values: bfloat16 [16384, 1024], P('ctx', 'tp')
- grad_square_mean: float32 [], replicated
Inputs may be any that keep to these rules, and one draw needn't show every extreme that they name: doc_start is non-decreasing, doc_start[p] <= p and p - doc_start[p] < 1024; a document is the run of tokens with equal doc_start, beginning at that position; at least one document holds exactly 1024 tokens; the last token forms a document of its own.
All inputs are finite; a program needn't handle non-finite values.
Results may differ from a plain program's by a relative error of at most 0.0086.
Values may be sent and summed in bfloat16 or wider, within the bound.
No kernel may reach another device: no remote copies, remote signals or barrier semaphores. Data moves between devices by JAX's collectives and lax.ppermute only.
A program may use at most 64 MiB of HBM per device.

v0:
```python
import jax
import jax.numpy as jnp
from jax import lax
from jax.sharding import PartitionSpec as P

HD = 128
REACH = 4


def shifted(x, axis, by):
    peers = lax.axis_size(axis)
    pairs = [(i, i + by) for i in range(peers) if 0 <= i + by < peers]
    return lax.ppermute(x, axis, pairs)


def shards(queries, keys, values, attn_out, grad_out, log_norm, doc_start):
    row_count = queries.shape[0]
    kv_count = keys.shape[1] // HD
    head_count = queries.shape[1] // HD
    group = head_count // kv_count
    scale = HD ** (-0.5)
    device = lax.axis_index("ctx")
    query_heads = queries.reshape(row_count, kv_count, group, HD)
    grad_heads = grad_out.reshape(row_count, kv_count, group, HD)
    out_heads = attn_out.reshape(row_count, kv_count, group, HD)
    delta = jnp.transpose(
        jnp.sum(grad_heads.astype(jnp.float32) * out_heads.astype(jnp.float32), axis=-1), (1, 2, 0)
    )
    norms = log_norm.reshape(kv_count, group, row_count)
    local_rows = jnp.arange(row_count, dtype=jnp.int32)
    query_pos = device * row_count + local_rows

    def tile_grads(offset, key_block, value_block):
        key_pos = (device - offset) * row_count + local_rows
        allowed = (key_pos[None, :] >= doc_start[:, None]) & (
            key_pos[None, :] <= query_pos[:, None]
        )
        scores = (
            jnp.einsum("ikgd,jkd->kgij", query_heads, key_block, preferred_element_type=jnp.float32)
            * scale
        )
        probs = jnp.where(allowed, jnp.exp(scores - norms[..., None]), 0.0)
        dprobs = jnp.einsum(
            "ikgd,jkd->kgij", grad_heads, value_block, preferred_element_type=jnp.float32
        )
        dscores = probs * (dprobs - delta[..., None])
        probs_low = probs.astype(jnp.bfloat16)
        dscores_low = dscores.astype(jnp.bfloat16)
        grad_v = jnp.einsum(
            "kgij,ikgd->jkd", probs_low, grad_heads, preferred_element_type=jnp.float32
        )
        grad_k = (
            jnp.einsum(
                "kgij,ikgd->jkd", dscores_low, query_heads, preferred_element_type=jnp.float32
            )
            * scale
        )
        grad_q = (
            jnp.einsum("kgij,jkd->ikgd", dscores_low, key_block, preferred_element_type=jnp.float32)
            * scale
        )
        return (grad_q, jnp.stack([grad_k, grad_v]))

    def guarded(offset, pair):
        key_block = pair[0].reshape(row_count, kv_count, HD)
        value_block = pair[1].reshape(row_count, kv_count, HD)
        return tile_grads(offset, key_block, value_block)

    kv_local = jnp.stack([keys, values])
    dq_total, own_part = guarded(0, kv_local)
    partials = []
    for offset in range(1, REACH + 1):
        arrived = shifted(kv_local, "ctx", offset)
        dq_part, kv_part = guarded(offset, arrived)
        dq_total = dq_total + dq_part
        partials.append(kv_part)
    grads = own_part
    for offset in range(1, REACH + 1):
        grads = grads + shifted(partials[offset - 1], "ctx", -offset)
    entry_total = float(row_count * lax.axis_size("ctx") * head_count * lax.axis_size("tp") * HD)
    grad_square_mean = lax.psum(jnp.sum(dq_total * dq_total) / entry_total, ("ctx", "tp"))
    grad_queries = dq_total.reshape(row_count, head_count * HD).astype(jnp.bfloat16)
    grad_keys = grads[0].reshape(row_count, kv_count * HD).astype(jnp.bfloat16)
    grad_values = grads[1].reshape(row_count, kv_count * HD).astype(jnp.bfloat16)
    return (grad_queries, grad_keys, grad_values, grad_square_mean)


def solution(mesh):
    return jax.shard_map(
        shards,
        mesh=mesh,
        in_specs=(
            P("ctx", "tp"),
            P("ctx", "tp"),
            P("ctx", "tp"),
            P("ctx", "tp"),
            P("ctx", "tp"),
            P("tp", "ctx"),
            P("ctx"),
        ),
        out_specs=(P("ctx", "tp"), P("ctx", "tp"), P("ctx", "tp"), P()),
        check_vma=False,
    )
```

profile of v0, /device:TPU:1, one launch (start us, length us, event | category | flops | bytes accessed | tf_op | source)
XLA Modules:
  0.0 183.7 jit_solution(3455858720892698083)
XLA Ops:
  0.6 0.0 copy-start
  0.6 1.6 pad_maximum_fusion.4
  2.3 4.4 %collective-permute-start.3 = (bf16[2,256,128]{2,1,0:T(8,128)(2,1)}, bf16[2,256,128]{2,1,0:T(8,128)(2,1)S(1)}, u32[]{:S(2)}, u32[]{:S(2)}) collective-permute-start(bf16[2,256,128]{2,1,0:T(8,128)(2,1)} %pad_maximum_fusion.4), channel_id=1, source_target_pairs={{0,32},{8,40},{16,48},{24,56},{32,64},{40,72},{48,80},{56,88},{64,... | collective-permute-start | bytes 393224 | tf_op jit(solution)/shard_map/ppermute | solution.py:13
  6.6 5.0 %collective-permute-start.2 = (bf16[2,256,128]{2,1,0:T(8,128)(2,1)}, bf16[2,256,128]{2,1,0:T(8,128)(2,1)}, u32[]{:S(2)}, u32[]{:S(2)}) collective-permute-start(bf16[2,256,128]{2,1,0:T(8,128)(2,1)} %pad_maximum_fusion.4), channel_id=1, source_target_pairs={{0,24},{8,32},{16,40},{24,48},{32,56},{40,64},{48,72},{56,80},{64,... | collective-permute-start | bytes 393224 | tf_op jit(solution)/shard_map/ppermute | solution.py:13
  11.7 4.4 %collective-permute-start.1 = (bf16[2,256,128]{2,1,0:T(8,128)(2,1)}, bf16[2,256,128]{2,1,0:T(8,128)(2,1)}, u32[]{:S(2)}, u32[]{:S(2)}) collective-permute-start(bf16[2,256,128]{2,1,0:T(8,128)(2,1)} %pad_maximum_fusion.4), channel_id=1, source_target_pairs={{0,16},{8,24},{16,32},{24,40},{32,48},{40,56},{48,64},{56,72},{64,... | collective-permute-start | bytes 393224 | tf_op jit(solution)/shard_map/ppermute | solution.py:13
  16.1 2.5 %collective-permute-start = (bf16[2,256,128]{2,1,0:T(8,128)(2,1)}, bf16[2,256,128]{2,1,0:T(8,128)(2,1)}, u32[]{:S(2)}, u32[]{:S(2)}) collective-permute-start(bf16[2,256,128]{2,1,0:T(8,128)(2,1)} %pad_maximum_fusion.4), channel_id=1, source_target_pairs={{0,8},{8,16},{16,24},{24,32},{32,40},{40,48},{48,56},{56,64},{64,7... | collective-permute-start | bytes 393224 | tf_op jit(solution)/shard_map/ppermute | solution.py:13
  18.6 0.6 iota_add_fusion.4
  19.2 1.9 %multiply_bitcast_fusion = f32[32,8,16,128]{3,1,2,0:T(8,128)S(1)} fusion(bf16[256,2048]{1,0:T(8,128)(2,1)} %param.10, bf16[256,2048]{1,0:T(8,128)(2,1)} %param.11), kind=kLoop, calls=%fused_computation.65 | loop fusion | flops 1572864 | bytes 4194304
  21.1 0.0 copy-start.3
  21.1 0.4 copy.91
  21.5 0.6 reduce_sum.20
  22.1 0.0 copy-start.2
  22.1 0.1 copy.44
  22.2 0.0 copy-done
  22.2 0.0 copy-done.3
  22.2 0.7 fusion.153
  22.9 0.0 copy-start.5
  22.9 0.0 copy-start.6
  23.0 1.1 compare_and_fusion
  24.1 0.0 copy-done.2
  24.1 2.4 %fusion.82 = f32[1,256,1,128]{3,1,2,0:T(8,128)} fusion(f32[256,256,16]{1,0,2:T(8,128)S(1)} %fusion.153, f32[16,256]{1,0:T(8,128)} %param.12, pred[256,256]{0,1:T(8,128)(4,1)S(1)} %get-tuple-element.19, bf16[256,2048]{1,0:T(8,128)(2,1)S(1)} %copy-done.2), kind=kOutput, calls=%fused_computation.80 | convolution fusion | flops 272629760 | bytes 5455872 | tf_op jit(solution)/shard_map/kgij,ikgd->jkd/dot_general | solution.py:49
  26.5 0.0 copy-done.5
  26.5 0.0 copy-done.6
  26.5 1.5 fusion.17
  28.0 0.5 fusion.51
  28.5 0.8 copy-done.1
  29.3 0.0 collective-permute-done
  29.3 1.5 fusion.151
  30.8 1.0 fusion.79
  31.9 2.3 %fusion.13 = bf16[1,16,256,256]{2,3,1,0:T(8,128)(2,1)S(1)} fusion(f32[256,256,16]{1,0,2:T(8,128)S(1)} %fusion.151, f32[16,256]{1,0:T(8,128)S(1)} %copy.44, f32[16,256]{1,0:T(8,128)S(1)} %copy-done.6, pred[256,256]{0,1:T(8,128)(4,1)S(1)} %get-tuple-element.20, bf16[2,256,128]{2,1,0:T(8,128)(2,1)} %collective-permute-done, bf16[256,2048]{1,0:T(8,128)(2,1)S(1)} %copy-done.2), kind=kOutput, calls=%fused_computation.20 | convolution fusion | flops 274726912 | bytes 7503872 | tf_op jit(solution)/shard_map/ikgd,jkd->kgij/dot_general | solution.py:43
  34.2 0.7 fusion.121
  35.0 1.5 collective-permute-start.4
  36.4 0.0 collective-permute-done.1
  36.4 1.6 fusion.149
  38.0 1.0 fusion.76
  39.0 2.3 %fusion.9 = bf16[1,16,256,256]{2,3,1,0:T(8,128)(2,1)S(1)} fusion(f32[256,256,16]{1,0,2:T(8,128)S(1)} %fusion.149, f32[16,256]{1,0:T(8,128)S(1)} %copy.44, f32[16,256]{1,0:T(8,128)S(1)} %copy-done.6, pred[256,256]{0,1:T(8,128)(4,1)S(1)} %get-tuple-element.17, bf16[2,256,128]{2,1,0:T(8,128)(2,1)} %collective-permute-done.1, bf16[256,2048]{1,0:T(8,128)(2,1)S(1)} %copy-done.2), kind=kOutput, calls=%fused_computation.14 | convolution fusion | flops 274726912 | bytes 7503872 | tf_op jit(solution)/shard_map/ikgd,jkd->kgij/dot_general | solution.py:43
  41.3 0.7 fusion.115
  42.1 1.3 collective-permute-start.5
  43.4 0.0 collective-permute-done.2
  43.4 1.6 fusion.147
  45.0 1.0 fusion.73
  46.0 2.3 %fusion.5 = bf16[1,16,256,256]{2,3,1,0:T(8,128)(2,1)S(1)} fusion(f32[256,256,16]{1,0,2:T(8,128)S(1)} %fusion.147, f32[16,256]{1,0:T(8,128)S(1)} %copy.44, f32[16,256]{1,0:T(8,128)S(1)} %copy-done.6, pred[256,256]{0,1:T(8,128)(4,1)S(1)} %get-tuple-element.18, bf16[2,256,128]{2,1,0:T(8,128)(2,1)} %collective-permute-done.2, bf16[256,2048]{1,0:T(8,128)(2,1)S(1)} %copy-done.2), kind=kOutput, calls=%fused_computation.8 | convolution fusion | flops 274726912 | bytes 7503872 | tf_op jit(solution)/shard_map/ikgd,jkd->kgij/dot_general | solution.py:43
  48.3 0.7 fusion.109
  49.1 1.3 collective-permute-start.6
  50.4 0.0 collective-permute-done.3
  50.4 0.7 fusion.145
  51.1 1.1 fusion.70
  52.2 1.5 fusion.1
  53.7 0.7 fusion.103
  54.4 1.5 collective-permute-start.7
  55.9 1.3 fusion.44
  57.2 1.3 fusion.40
  58.6 1.3 fusion.36
  59.9 1.8 multiply_reduce_fusion
  62.4 2.9 %fusion.127 = f32[1,256,1,128]{3,1,2,0:T(8,128)} fusion(bf16[1,16,256,256]{2,3,1,0:T(8,128)(2,1)} %copy-done.1, bf16[256,2048]{1,0:T(8,128)(2,1)S(1)} %copy-done), kind=kOutput, calls=%fused_computation.95 | convolution fusion | flops 268468224 | bytes 3276800 | tf_op jit(solution)/shard_map/kgij,ikgd->jkd/dot_general | solution.py:53
  65.3 115.0 %psum.7 = f32[]{:T(128)} all-reduce(f32[]{:T(128)S(6)} %div.3), channel_id=1, replica_groups=mesh['ctx'=64,'tp'=8] {'ctx','tp'}, use_global_device_ids=true, to_apply=%region_2.3 | all-reduce | flops 1 | bytes 8 | tf_op jit(solution)/shard_map/psum | solution.py:81
  180.4 1.4 copy.73
  181.8 0.0 collective-permute-done.4
  181.8 0.0 collective-permute-done.5
  181.8 0.0 collective-permute-done.6
  181.8 0.0 collective-permute-done.7
  181.8 0.0 copy-done.4
  181.8 1.2 fusion.158
  183.0 0.7 slice_bitcast_fusion
  (8 shorter events, 0.1 us)
Async XLA Ops:
  0.6 21.6 %copy-start = (bf16[256,2048]{1,0:T(8,128)(2,1)S(1)}, bf16[256,2048]{1,0:T(8,128)(2,1)}, u32[]{:S(2)}) copy-start(bf16[256,2048]{1,0:T(8,128)(2,1)} %param.7) | copy-start | bytes 3145732
  2.3 48.1 %collective-permute-start.3 = (bf16[2,256,128]{2,1,0:T(8,128)(2,1)}, bf16[2,256,128]{2,1,0:T(8,128)(2,1)S(1)}, u32[]{:S(2)}, u32[]{:S(2)}) collective-permute-start(bf16[2,256,128]{2,1,0:T(8,128)(2,1)} %pad_maximum_fusion.4), channel_id=1, source_target_pairs={{0,32},{8,40},{16,48},{24,56},{32,64},{40,72},{48,80},{56,88},{64,... | collective-permute-start | bytes 393224 | tf_op jit(solution)/shard_map/ppermute | solution.py:13
  6.6 36.8 %collective-permute-start.2 = (bf16[2,256,128]{2,1,0:T(8,128)(2,1)}, bf16[2,256,128]{2,1,0:T(8,128)(2,1)}, u32[]{:S(2)}, u32[]{:S(2)}) collective-permute-start(bf16[2,256,128]{2,1,0:T(8,128)(2,1)} %pad_maximum_fusion.4), channel_id=1, source_target_pairs={{0,24},{8,32},{16,40},{24,48},{32,56},{40,64},{48,72},{56,80},{64,... | collective-permute-start | bytes 393224 | tf_op jit(solution)/shard_map/ppermute | solution.py:13
  11.7 24.7 %collective-permute-start.1 = (bf16[2,256,128]{2,1,0:T(8,128)(2,1)}, bf16[2,256,128]{2,1,0:T(8,128)(2,1)}, u32[]{:S(2)}, u32[]{:S(2)}) collective-permute-start(bf16[2,256,128]{2,1,0:T(8,128)(2,1)} %pad_maximum_fusion.4), channel_id=1, source_target_pairs={{0,16},{8,24},{16,32},{24,40},{32,48},{40,56},{48,64},{56,72},{64,... | collective-permute-start | bytes 393224 | tf_op jit(solution)/shard_map/ppermute | solution.py:13
  16.1 13.2 %collective-permute-start = (bf16[2,256,128]{2,1,0:T(8,128)(2,1)}, bf16[2,256,128]{2,1,0:T(8,128)(2,1)}, u32[]{:S(2)}, u32[]{:S(2)}) collective-permute-start(bf16[2,256,128]{2,1,0:T(8,128)(2,1)} %pad_maximum_fusion.4), channel_id=1, source_target_pairs={{0,8},{8,16},{16,24},{24,32},{32,40},{40,48},{48,56},{56,64},{64,7... | collective-permute-start | bytes 393224 | tf_op jit(solution)/shard_map/ppermute | solution.py:13
  21.1 1.1 copy-start.3
  22.1 1.9 %copy-start.2 = (bf16[256,2048]{1,0:T(8,128)(2,1)S(1)}, bf16[256,2048]{1,0:T(8,128)(2,1)}, u32[]{:S(2)}) copy-start(bf16[256,2048]{1,0:T(8,128)(2,1)} %param.11) | copy-start | bytes 3145732
  22.9 3.6 %copy-start.5 = (bf16[256,128]{1,0:T(8,128)(2,1)S(1)}, bf16[256,128]{1,0:T(8,128)(2,1)}, u32[]{:S(2)}) copy-start(bf16[256,128]{1,0:T(8,128)(2,1)} %param.9) | copy-start | bytes 196612
  22.9 3.6 %copy-start.6 = (f32[16,256]{1,0:T(8,128)S(1)}, f32[16,256]{1,0:T(8,128)}, u32[]{:S(2)}) copy-start(f32[16,256]{1,0:T(8,128)} %param.12) | copy-start | bytes 49156
  28.0 1.3 copy-start.1
  35.0 146.8 %collective-permute-start.4 = (f32[2,256,1,128]{3,1,2,0:T(8,128)S(1)}, f32[2,256,1,128]{3,1,2,0:T(8,128)S(1)}, u32[]{:S(2)}, u32[]{:S(2)}) collective-permute-start(f32[2,256,1,128]{3,1,2,0:T(8,128)S(1)} %pad_maximum_fusion), channel_id=1, source_target_pairs={{8,0},{16,8},{24,16},{32,24},{40,32},{48,40},{56,48},{64,56},{72,6... | collective-permute-start | bytes 786440 | tf_op jit(solution)/shard_map/ppermute | solution.py:13
  42.1 139.7 %collective-permute-start.5 = (f32[2,256,1,128]{3,1,2,0:T(8,128)S(1)}, f32[2,256,1,128]{3,1,2,0:T(8,128)}, u32[]{:S(2)}, u32[]{:S(2)}) collective-permute-start(f32[2,256,1,128]{3,1,2,0:T(8,128)S(1)} %pad_maximum_fusion.1), channel_id=1, source_target_pairs={{16,0},{24,8},{32,16},{40,24},{48,32},{56,40},{64,48},{72,56},{80,... | collective-permute-start | bytes 786440 | tf_op jit(solution)/shard_map/ppermute | solution.py:13
  49.1 132.7 %collective-permute-start.6 = (f32[2,256,1,128]{3,1,2,0:T(8,128)S(1)}, f32[2,256,1,128]{3,1,2,0:T(8,128)}, u32[]{:S(2)}, u32[]{:S(2)}) collective-permute-start(f32[2,256,1,128]{3,1,2,0:T(8,128)S(1)} %pad_maximum_fusion.2), channel_id=1, source_target_pairs={{24,0},{32,8},{40,16},{48,24},{56,32},{64,40},{72,48},{80,56},{88,... | collective-permute-start | bytes 786440 | tf_op jit(solution)/shard_map/ppermute | solution.py:13
  54.4 127.4 %collective-permute-start.7 = (f32[2,256,1,128]{3,1,2,0:T(8,128)S(1)}, f32[2,256,1,128]{3,1,2,0:T(8,128)}, u32[]{:S(2)}, u32[]{:S(2)}) collective-permute-start(f32[2,256,1,128]{3,1,2,0:T(8,128)S(1)} %pad_maximum_fusion.3), channel_id=1, source_target_pairs={{32,0},{40,8},{48,16},{56,24},{64,32},{72,40},{80,48},{88,56},{96,... | collective-permute-start | bytes 786440 | tf_op jit(solution)/shard_map/ppermute | solution.py:13
  61.7 120.1 %copy-start.4 = (f32[1,256,1,128]{3,1,2,0:T(8,128)S(1)}, f32[1,256,1,128]{3,1,2,0:T(8,128)}, u32[]{:S(2)}) copy-start(f32[1,256,1,128]{3,1,2,0:T(8,128)} %fusion.82) | copy-start | bytes 393220
where the time goes:
time: 185 us; the launch traced here: 184 us
  blocking collectives  115 us (62%)
  matrix products  34.6 us (19%)
  starting transfers between devices  21.9 us (12%)
  other arithmetic  7.07 us (4%)
  local copies, waits for them, and re-layouts  3.39 us (2%)
    psum x1, blocking collectives, shards(): lax.psum(jnp.sum(dq_total * dq_total) / entry_total, ('ctx', 'tp'))  115 us
    ppermute x8, starting transfers between devices, shifted(): return lax.ppermute(x, axis, pairs)  21.9 us
    dot_general x5, matrix products, tile_grads(): jnp.einsum('ikgd,jkd->kgij', grad_heads, value_block, preferred_element_t...  9.8 us
    dot_general x5, matrix products, tile_grads(): jnp.einsum('kgij,ikgd->jkd', probs_low, grad_heads, preferred_element_typ...  6.61 us
    dot_general x5, matrix products, tile_grads(): jnp.einsum('kgij,jkd->ikgd', dscores_low, key_block, preferred_element_ty...  6.24 us
    dot_general x5, matrix products, tile_grads(): jnp.einsum('ikgd,jkd->kgij', query_heads, key_block, preferred_element_ty...  6.08 us
    dot_general x5, matrix products, tile_grads(): jnp.einsum('kgij,ikgd->jkd', dscores_low, query_heads, preferred_element_...  5.86 us
  transfers between devices with their start and end apart: 8, of which 0 were waited for; matrix products, arithmetic and copies ran while one was open for 22% of the time, Pallas kernels for 0%

commit v1 on v0

v1 whole, which is shorter than its diff:
```python
import functools
import math

import jax
import jax.numpy as jnp
from jax import lax
from jax.experimental import pallas as pl
from jax.experimental.pallas import tpu as pltpu
from jax.sharding import PartitionSpec as P

HD = 128
ROWS = 256
HEADS = 16
REACH = 4
ROW_X = 4
LOG2E = math.log2(math.e)
SCALE = HD**-0.5
NT = (((1,), (1,)), ((), ()))
NN = (((1,), (0,)), ((), ()))
BF16 = jnp.bfloat16
F32 = jnp.float32


def dot(a, b, dims=NN):
    return lax.dot_general(a, b, dims, preferred_element_type=F32)


def columns(h):
    return slice(h * HD, (h + 1) * HD)


def rows_of(h):
    return slice(h * ROWS, (h + 1) * ROWS)


def pieces(x):
    first = x.astype(BF16).astype(F32)
    rest = x - first
    second = rest.astype(BF16).astype(F32)
    return first, second, (rest - second).astype(BF16).astype(F32)


def prepare_kernel(q, g, o, norm, q_t, g_t, ext, ext_t):
    ones = jnp.ones((8, HD), BF16)
    place = lax.broadcasted_iota(jnp.int32, (8, ROWS), 0)
    for h in range(HEADS):
        q_t[:, rows_of(h)] = q[:, columns(h)].T
        g_t[:, rows_of(h)] = g[:, columns(h)].T
        product = g[:, columns(h)].astype(F32) * o[:, columns(h)].astype(F32)
        high = product.astype(BF16)
        low = (product - high.astype(F32)).astype(BF16)
        delta = dot(ones, high, NT) + dot(ones, low, NT)
        shift = jnp.broadcast_to(norm[h : h + 1, :] * (-(HD**0.5)), (8, ROWS))
        block = jnp.zeros((8, ROWS), F32)
        for r, term in enumerate(pieces(shift) + pieces(-delta)):
            block = jnp.where(place == r, term, block)
        ext_t[8 * h : 8 * h + 8, :] = block
    ext[...] = ext_t[...].T.astype(BF16)


def tile_grads(q, g, q_t, g_t, ext, k, v, bias, dq, dkv):
    lane = lax.broadcasted_iota(jnp.int32, (ROWS, HD), 1)
    k_wide = jnp.concatenate([k, jnp.where(lane % 8 < 3, 1.0, 0.0).astype(BF16)], axis=1)
    v_wide = jnp.concatenate([v, jnp.where((lane % 8 >= 3) & (lane % 8 < 6), 1.0, 0.0).astype(BF16)], axis=1)
    extras = [jnp.where(lane // 8 == h, ext[...], jnp.zeros((), BF16)) for h in range(HEADS)]
    q_wide = jnp.concatenate([jnp.concatenate([q[:, columns(h)], extras[h]], axis=1) for h in range(HEADS)], axis=0)
    g_wide = jnp.concatenate([jnp.concatenate([g[:, columns(h)], extras[h]], axis=1) for h in range(HEADS)], axis=0)
    scores = dot(q_wide, k_wide, NT)
    dprobs = dot(g_wide, v_wide, NT)
    probs = jnp.exp2(scores * (SCALE * LOG2E) + jnp.concatenate([bias[...]] * HEADS, axis=0))
    dscores = (probs * dprobs).astype(BF16)
    dq[...] += dot(dscores, k)
    dkv[:, :ROWS] = dot(q_t[...], dscores) * SCALE
    dkv[:, ROWS:] = dot(g_t[...], probs.astype(BF16))


def set_bias(bias, doc, ctx, offset):
    key_pos = (ctx - offset) * ROWS + lax.broadcasted_iota(jnp.int32, (ROWS, ROWS), 1)
    query_pos = ctx * ROWS + lax.broadcasted_iota(jnp.int32, (ROWS, ROWS), 0)
    bias[...] = jnp.where((key_pos >= doc[...]) & (key_pos <= query_pos), 0.0, -1e30)


def near_kernel(meta, doc, q, g, q_t, g_t, ext, own, far, dq, own_grads, far_grads, bias, dkv):
    ctx, first = meta[0], meta[1]
    dq[...] = jnp.zeros_like(dq)
    far_grads[...] = jnp.zeros_like(far_grads)
    set_bias(bias, doc, ctx, 0)
    tile_grads(q, g, q_t, g_t, ext, own[:ROWS], own[ROWS:], bias, dq, dkv)
    own_grads[:ROWS] = dkv[:, :ROWS].T
    own_grads[ROWS:] = dkv[:, ROWS:].T

    @pl.when(first < (ctx - REACH + 1) * ROWS)
    def _():
        set_bias(bias, doc, ctx, REACH)
        tile_grads(q, g, q_t, g_t, ext, far[:ROWS], far[ROWS:], bias, dq, dkv)
        far_grads[:ROWS] = dkv[:, :ROWS].T.astype(BF16)
        far_grads[ROWS:] = dkv[:, ROWS:].T.astype(BF16)


def between_kernel(meta, doc, q, g, q_t, g_t, ext, blocks, dq_in, far_grads, dq, squares, parts, total, bias, dkv):
    ctx, first = meta[0], meta[1]
    x = lax.rem(ctx, ROW_X)
    total[...] = dq_in[...]
    parts[...] = jnp.zeros_like(parts)
    parts[x] = far_grads[...]
    reach = jnp.clip(lax.div(ctx * ROWS - first + (ROWS - 1), ROWS), 0, REACH - 1)

    def one(offset, carry):
        slot = lax.rem(x - offset + ROW_X, ROW_X)
        set_bias(bias, doc, ctx, offset)
        tile_grads(q, g, q_t, g_t, ext, blocks[slot, :ROWS], blocks[slot, ROWS:], bias, total, dkv)
        parts[slot, :ROWS] = dkv[:, :ROWS].T.astype(BF16)
        parts[slot, ROWS:] = dkv[:, ROWS:].T.astype(BF16)
        return carry

    lax.fori_loop(1, reach + 1, one, 0)
    square = jnp.zeros((8, HD), F32)
    for h in range(HEADS):
        block = total[rows_of(h), :] * SCALE
        dq[:, columns(h)] = block.astype(BF16)
        square += jnp.sum((block * block).reshape(ROWS // 8, 8, HD), axis=0)
    squares[...] = jnp.broadcast_to(jnp.sum(square, axis=0, keepdims=True), (8, HD))


VMEM = pl.BlockSpec(memory_space=pltpu.VMEM)
SMEM = pl.BlockSpec(memory_space=pltpu.SMEM)


def call(kernel, outs, scratch, args, smem=0, limit=24, tiles=0.0):
    return pl.pallas_call(
        kernel,
        out_shape=tuple(jax.ShapeDtypeStruct(shape, dtype) for shape, dtype in outs),
        in_specs=[SMEM] * smem + [VMEM] * (len(args) - smem),
        out_specs=(VMEM,) * len(outs),
        scratch_shapes=[pltpu.VMEM(shape, dtype) for shape, dtype in scratch],
        compiler_params=pltpu.CompilerParams(vmem_limit_bytes=limit * 2**20),
        cost_estimate=pl.CostEstimate(
            flops=int(tiles * 10 * HEADS * ROWS * ROWS * HD), bytes_accessed=4 * 2**20, transcendentals=0
        ),
    )(*args)


def exchange_x(x):
    groups = [[z * ROW_X + i for i in range(ROW_X)] for z in range(lax.axis_size("ctx") // ROW_X)]
    return lax.all_to_all(x, "ctx", 0, 0, axis_index_groups=groups, tiled=True)


def shift_z(x, by):
    peers = lax.axis_size("ctx")
    return lax.ppermute(x, "ctx", [(i, (i + ROW_X * by) % peers) for i in range(peers)])


def shards(queries, keys, values, attn_out, grad_out, log_norm, doc_start):
    ctx = lax.axis_index("ctx")
    x = lax.rem(ctx, ROW_X)
    wide = ROWS * HEADS
    slots = jnp.arange(ROW_X, dtype=jnp.int32)[:, None, None]

    own = jnp.concatenate([keys, values], axis=0)
    far = shift_z(own, 1)
    meta = jnp.stack([ctx, doc_start[0]])
    doc = doc_start.reshape(ROWS, 1)
    q_t, g_t, ext = call(
        prepare_kernel,
        [((HD, wide), BF16), ((HD, wide), BF16), ((ROWS, HD), BF16)],
        [((HD, ROWS), F32)],
        (queries, grad_out, attn_out, log_norm),
        tiles=1.0,
    )
    far, q_t, g_t, ext = lax.optimization_barrier((far, q_t, g_t, ext))
    blocks = exchange_x(jnp.where(slots > x, own[None], far[None]))
    common = (meta, doc, queries, grad_out, q_t, g_t, ext)
    tile_scratch = [((ROWS, ROWS), F32), ((HD, 2 * ROWS), F32)]
    dq_near, own_grads, far_grads = call(
        near_kernel,
        [((wide, HD), F32), ((2 * ROWS, HD), F32), ((2 * ROWS, HD), BF16)],
        tile_scratch,
        common + (own, far),
        smem=1,
        tiles=2.0,
    )
    blocks, dq_near, own_grads, far_grads = lax.optimization_barrier((blocks, dq_near, own_grads, far_grads))
    grad_queries, squares, parts = call(
        between_kernel,
        [((ROWS, HEADS * HD), BF16), ((8, HD), F32), ((ROW_X, 2 * ROWS, HD), BF16)],
        [((wide, HD), F32)] + tile_scratch,
        common + (blocks, dq_near, far_grads),
        smem=1,
        tiles=3.0,
    )

    squares_tp = lax.all_to_all(squares, "tp", 0, 0, tiled=True)
    back = exchange_x(parts)
    peers = lax.axis_size("ctx")
    row = jnp.sum(squares_tp, axis=0, keepdims=True)
    squares_ctx = lax.all_to_all(jnp.broadcast_to(row, (peers, HD)), "ctx", 0, 0, tiled=True)
    back = back.astype(F32)
    onward = jnp.sum(jnp.where(slots <= x, back, 0.0), axis=0).astype(BF16)
    mine = jnp.sum(jnp.where(slots > x, back, 0.0), axis=0)
    grads = own_grads + mine + shift_z(onward, -1).astype(F32)
    entries = float(ROWS * peers * HEADS * lax.axis_size("tp") * HD)
    grad_square_mean = jnp.sum(squares_ctx) / entries
    grads = grads.astype(BF16)
    return (grad_queries, grads[:ROWS], grads[ROWS:], grad_square_mean)


def solution(mesh):
    return jax.shard_map(
        shards,
        mesh=mesh,
        in_specs=(
            P("ctx", "tp"),
            P("ctx", "tp"),
            P("ctx", "tp"),
            P("ctx", "tp"),
            P("ctx", "tp"),
            P("tp", "ctx"),
            P("ctx"),
        ),
        out_specs=(P("ctx", "tp"), P("ctx", "tp"), P("ctx", "tp"), P()),
        check_vma=False,
    )
```

time: 185 us -> 98 us (0.53)
  blocking collectives: 115 us -> 24.6 us
  matrix products: 34.6 us -> 0 us
  local copies, waits for them, and re-layouts: 3.39 us -> 17.2 us
  starting transfers between devices: 21.9 us -> 33.4 us
  waiting for transfers between devices: 0.02 us -> 10.7 us
  Pallas kernels: 0 us -> 6.14 us
  other arithmetic: 7.07 us -> 2.61 us
    psum x1 -> x0, blocking collectives: 115 us -> none  [shards(): lax.psum(jnp.sum(dq_total * dq_total) / entry_total, ('ctx', 'tp'))]
    dot_general x25 -> x0, matrix products: 34.6 us -> none  [the longest x5 9.8 us: tile_grads(): jnp.einsum('ikgd,jkd->kgij', grad_heads, value_block, preferred_element_t...]
    all_to_all x0 -> x1, blocking collectives: none -> 24.6 us  [shards(): lax.all_to_all(jnp.broadcast_to(row, (peers, HD)), 'ctx', 0, 0, tiled=True)]
    all_to_all x0 -> x3, starting transfers between devices: none -> 23.1 us  [the longest x2 15.3 us: exchange_x(): return lax.all_to_all(x, 'ctx', 0, 0, axis_index_groups=groups, tiled=True)]
    unnamed x16 -> x31, local copies, waits for them, and re-layouts: 2.67 us -> 15 us
    ppermute x8 -> x2, starting transfers between devices: 21.9 us -> 10.4 us  [shift_z(): lax.ppermute(x, 'ctx', [(i, (i + ROW_X * by) % peers) for i in range(peer...]
    all_to_all x0 -> x3, waiting for transfers between devices: none -> 7.15 us  [the longest x2 7.14 us: exchange_x(): return lax.all_to_all(x, 'ctx', 0, 0, axis_index_groups=groups, tiled=True)]
    pallas_call x0 -> x3, Pallas kernels: none -> 6.14 us  [call(): pl.pallas_call(kernel, out_shape=tuple((jax.ShapeDtypeStruct(shape, dtype...]
  transfers between devices with their start and end apart: 8 -> 5, of which waited for: 0 -> 2; matrix products, arithmetic and copies ran while one was open for 22% -> 2% of each run, Pallas kernels for 0% -> 4%
where the time goes in v1:
time: 98 us; the launch traced here: 97.2 us
  starting transfers between devices  33.4 us (34%)
  blocking collectives  24.6 us (25%)
  local copies, waits for them, and re-layouts  17.2 us (18%)
  waiting for transfers between devices  10.7 us (11%)
  Pallas kernels  6.14 us (6%)
  other arithmetic  2.61 us (3%)
  between operations  2.54 us (3%)
    all_to_all x1, blocking collectives, shards(): lax.all_to_all(jnp.broadcast_to(row, (peers, HD)), 'ctx', 0, 0, tiled=True)  24.6 us
    all_to_all x2, starting transfers between devices, exchange_x(): return lax.all_to_all(x, 'ctx', 0, 0, axis_index_groups=groups, tiled=True)  15.3 us
    unnamed x31, local copies, waits for them, and re-layouts  15 us
    ppermute x2, starting transfers between devices, shift_z(): lax.ppermute(x, 'ctx', [(i, (i + ROW_X * by) % peers) for i in range(peer...  10.4 us
    all_to_all x1, starting transfers between devices, shards(): squares_tp = lax.all_to_all(squares, 'tp', 0, 0, tiled=True)  7.75 us
    all_to_all x2, waiting for transfers between devices, exchange_x(): return lax.all_to_all(x, 'ctx', 0, 0, axis_index_groups=groups, tiled=True)  7.14 us
    pallas_call x3, Pallas kernels, call(): pl.pallas_call(kernel, out_shape=tuple((jax.ShapeDtypeStruct(shape, dtype...  6.14 us
    ppermute x2, waiting for transfers between devices, shift_z(): lax.ppermute(x, 'ctx', [(i, (i + ROW_X * by) % peers) for i in range(peer...  3.53 us
  transfers between devices with their start and end apart: 5, of which 2 were waited for; matrix products, arithmetic and copies ran while one was open for 2% of the time, Pallas kernels for 4%

profile of v1, /device:TPU:1, one launch (start us, length us, event | category | flops | bytes accessed | tf_op | source)
XLA Modules:
  0.0 97.2 jit_solution(16236505490065990553)
XLA Ops:
  0.6 0.8 constant_dynamic-update-slice_fusion.1
  1.5 0.9 constant_dynamic-update-slice_fusion.own
  2.3 4.4 %collective-permute-start = (bf16[512,128]{1,0:T(8,128)(2,1)S(1)}, bf16[512,128]{1,0:T(8,128)(2,1)S(1)}, u32[]{:S(2)}, u32[]{:S(2)}) collective-permute-start(bf16[512,128]{1,0:T(8,128)(2,1)S(1)} %constant_dynamic-update-slice_fusion.own), channel_id=1, source_target_pairs={{0,32},{8,40},{16,48},{24,56},{32,64},{40,72},{48,80},{56,88},{64,... | collective-permute-start | bytes 393224 | tf_op jit(solution)/shard_map/ppermute | solution.py:150
  6.7 0.0 copy-start
  6.7 1.2 %copy-done = bf16[256,2048]{1,0:T(8,128)(2,1)S(1)} copy-done((bf16[256,2048]{1,0:T(8,128)(2,1)S(1)}, bf16[256,2048]{1,0:T(8,128)(2,1)}, u32[]{:S(2)}) %copy-start) | copy-done | bytes 1048600
  8.0 0.0 copy-start.1
  8.0 1.2 %copy-done.1 = bf16[256,2048]{1,0:T(8,128)(2,1)S(1)} copy-done((bf16[256,2048]{1,0:T(8,128)(2,1)S(1)}, bf16[256,2048]{1,0:T(8,128)(2,1)}, u32[]{:S(2)}) %copy-start.1) | copy-done | bytes 1048600
  9.2 0.0 copy-start.3
  9.2 1.2 %copy-done.3 = bf16[256,2048]{1,0:T(8,128)(2,1)S(1)} copy-done((bf16[256,2048]{1,0:T(8,128)(2,1)S(1)}, bf16[256,2048]{1,0:T(8,128)(2,1)}, u32[]{:S(2)}) %copy-start.3) | copy-done | bytes 1048600
  10.4 0.0 copy-start.5
  10.4 0.7 copy-done.5
  11.1 0.0 copy-start.14
  11.1 0.0 copy-start.2
  11.1 0.0 copy-start.4
  11.1 0.9 shard_map.102
  12.0 0.0 copy-start.6
  12.0 1.0 copy-done.6
  13.0 0.0 copy-start.9
  13.0 1.0 copy-done.9
  14.0 3.5 %collective-permute-done.far = bf16[512,128]{1,0:T(8,128)(2,1)S(1)} collective-permute-done((bf16[512,128]{1,0:T(8,128)(2,1)S(1)}, bf16[512,128]{1,0:T(8,128)(2,1)S(1)}, u32[]{:S(2)}, u32[]{:S(2)}) %collective-permute-start) | collective-permute-done | bytes 131104 | tf_op jit(solution)/shard_map/ppermute | solution.py:150
  17.5 0.9 broadcast_select_fusion
  18.4 4.0 %all-to-all-start = ((bf16[4,512,128]{2,1,0:T(8,128)(2,1)}), bf16[4,512,128]{2,1,0:T(8,128)(2,1)S(1)}, u32[]{:S(2)}, u32[]{:S(2)}) async-start(bf16[4,512,128]{2,1,0:T(8,128)(2,1)} %broadcast_select_fusion), calls=%async_computation | async-start | bytes 1048576 | tf_op jit(solution)/shard_map/all_to_all | solution.py:145
  22.4 0.0 copy-done.14
  22.4 0.5 slice.9
  22.9 0.1 copy.20.doc
  23.1 0.7 pad_add_fusion.meta
  23.8 0.0 copy-done.2
  23.8 0.0 copy-done.4
  23.8 0.0 copy-start.7
  23.8 1.2 %copy-done.7 = bf16[128,4096]{1,0:T(8,128)(2,1)S(1)} copy-done((bf16[128,4096]{1,0:T(8,128)(2,1)S(1)}, bf16[128,4096]{1,0:T(8,128)(2,1)}, u32[]{:S(2)}) %copy-start.7) | copy-done | bytes 1048600
  25.0 0.0 copy-start.10
  25.0 1.2 %copy-done.10 = bf16[128,4096]{1,0:T(8,128)(2,1)S(1)} copy-done((bf16[128,4096]{1,0:T(8,128)(2,1)S(1)}, bf16[128,4096]{1,0:T(8,128)(2,1)}, u32[]{:S(2)}) %copy-start.10) | copy-done | bytes 1048600
  26.2 3.0 %shard_map.103 = (f32[4096,128]{1,0:T(8,128)S(1)}, f32[512,128]{1,0:T(8,128)S(1)}, bf16[512,128]{1,0:T(8,128)(2,1)S(1)}) custom-call(s32[2]{0:T(128)S(1)} %pad_add_fusion.meta, s32[256,1]{1,0:T(8,128)S(1)} %copy.20.doc, bf16[256,2048]{1,0:T(8,128)(2,1)S(1)} %copy-done.2, bf16[256,2048]{1,0:T(8,128)(2,1)S(1)} %copy-done.4, bf16[128,4096]{1,0:T(8,128)(2,1)S(1)} %copy-done.7, ...), custom_call_target="tpu_custom_call" | custom-call | flops 2684354560 | bytes 4194304 | tf_op jit(solution)/shard_map/pallas_call | solution.py:130
  29.2 0.0 copy-start.12
  29.3 1.3 %copy-done.12 = f32[4096,128]{1,0:T(8,128)} copy-done((f32[4096,128]{1,0:T(8,128)}, f32[4096,128]{1,0:T(8,128)S(1)}, u32[]{:S(2)}) %copy-start.12) | copy-done | bytes 2097176
  30.6 0.0 all-to-all-done.blocks
  30.6 0.0 copy-start.8
  30.6 1.2 %copy-done.8 = bf16[128,4096]{1,0:T(8,128)(2,1)S(1)} copy-done((bf16[128,4096]{1,0:T(8,128)(2,1)S(1)}, bf16[128,4096]{1,0:T(8,128)(2,1)}, u32[]{:S(2)}) %copy-start.8) | copy-done | bytes 1048600
  31.8 0.0 copy-start.11
  31.8 1.2 %copy-done.11 = bf16[128,4096]{1,0:T(8,128)(2,1)S(1)} copy-done((bf16[128,4096]{1,0:T(8,128)(2,1)S(1)}, bf16[128,4096]{1,0:T(8,128)(2,1)}, u32[]{:S(2)}) %copy-start.11) | copy-done | bytes 1048600
  33.0 0.0 copy-start.13
  33.0 1.6 %copy-done.13 = f32[4096,128]{1,0:T(8,128)S(1)} copy-done((f32[4096,128]{1,0:T(8,128)S(1)}, f32[4096,128]{1,0:T(8,128)}, u32[]{:S(2)}) %copy-start.13) | copy-done | bytes 2097176
  34.6 2.3 %shard_map.104 = (bf16[256,2048]{1,0:T(8,128)(2,1)}, f32[8,128]{1,0:T(8,128)}, bf16[4,512,128]{2,1,0:T(8,128)(2,1)}) custom-call(s32[2]{0:T(128)S(1)} %pad_add_fusion.meta, s32[256,1]{1,0:T(8,128)S(1)} %copy.20.doc, bf16[256,2048]{1,0:T(8,128)(2,1)S(1)} %copy-done.2, bf16[256,2048]{1,0:T(8,128)(2,1)S(1)} %copy-done.4, bf16[128,4096]{1,0:T(8,128)(2,1)S(1)} %copy-done.8, ...), custom_call_target="tpu_custom_call" | custom-call | flops 4026531840 | bytes 4194304 | tf_op jit(solution)/shard_map/pallas_call | solution.py:130
  36.9 11.3 %all-to-all-start.1 = ((bf16[4,512,128]{2,1,0:T(8,128)(2,1)}), bf16[4,512,128]{2,1,0:T(8,128)(2,1)S(1)}, u32[]{:S(2)}, u32[]{:S(2)}) async-start(bf16[4,512,128]{2,1,0:T(8,128)(2,1)} %get-tuple-element.36), calls=%async_computation.1 | async-start | bytes 1048576 | tf_op jit(solution)/shard_map/all_to_all | solution.py:145
  48.2 7.1 %all-to-all-done.1 = bf16[4,512,128]{2,1,0:T(8,128)(2,1)S(1)} async-done(((bf16[4,512,128]{2,1,0:T(8,128)(2,1)}), bf16[4,512,128]{2,1,0:T(8,128)(2,1)S(1)}, u32[]{:S(2)}, u32[]{:S(2)}) %all-to-all-start.1) | async-done | bytes 524320 | tf_op jit(solution)/shard_map/all_to_all | solution.py:145
  55.4 7.7 %all-to-all-start.2 = ((f32[8,1,128]{2,1,0:T(1,128)}), f32[8,1,128]{2,1,0:T(1,128)S(1)}, u32[]{:S(2)}, u32[]{:S(2)}) async-start(f32[8,1,128]{2,1,0:T(1,128)} %bitcast.3), calls=%async_computation.2 | async-start | bytes 8192 | tf_op jit(solution)/shard_map/all_to_all | solution.py:192
  63.1 0.3 fusion
  63.4 6.0 %collective-permute-start.1 = (bf16[512,128]{1,0:T(8,128)(2,1)S(1)}, bf16[512,128]{1,0:T(8,128)(2,1)S(1)}, u32[]{:S(2)}, u32[]{:S(2)}) collective-permute-start(bf16[512,128]{1,0:T(8,128)(2,1)S(1)} %get-tuple-element.39), channel_id=1, source_target_pairs={{0,480},{8,488},{16,496},{24,504},{32,0},{40,8},{48,16},{56,24},{6... | collective-permute-start | bytes 393224 | tf_op jit(solution)/shard_map/ppermute | solution.py:150
  69.4 0.0 all-to-all-done.2
  69.5 24.6 %all_to_all.25 = f32[64,1,128]{2,1,0:T(1,128)S(1)} all-to-all(f32[64,1,128]{2,1,0:T(1,128)S(1)} %broadcast_in_dim.54), channel_id=1, replica_groups=mesh['ctx'=64,'tp'=8] {'ctx'}, dimensions={0} | all-to-all | bytes 65536 | tf_op jit(solution)/shard_map/all_to_all | solution.py:196
  94.0 0.6 reduce_sum.39
  95.3 0.0 collective-permute-done.1
  95.4 0.7 fusion.2
  (5 shorter events, 0.1 us)
Async XLA Ops:
  2.3 15.2 %collective-permute-start = (bf16[512,128]{1,0:T(8,128)(2,1)S(1)}, bf16[512,128]{1,0:T(8,128)(2,1)S(1)}, u32[]{:S(2)}, u32[]{:S(2)}) collective-permute-start(bf16[512,128]{1,0:T(8,128)(2,1)S(1)} %constant_dynamic-update-slice_fusion.own), channel_id=1, source_target_pairs={{0,32},{8,40},{16,48},{24,56},{32,64},{40,72},{48,80},{56,88},{64,... | collective-permute-start | bytes 393224 | tf_op jit(solution)/shard_map/ppermute | solution.py:150
  6.7 1.2 %copy-start = (bf16[256,2048]{1,0:T(8,128)(2,1)S(1)}, bf16[256,2048]{1,0:T(8,128)(2,1)}, u32[]{:S(2)}) copy-start(bf16[256,2048]{1,0:T(8,128)(2,1)} %o.1) | copy-start | bytes 3145732
  8.0 1.2 %copy-start.1 = (bf16[256,2048]{1,0:T(8,128)(2,1)S(1)}, bf16[256,2048]{1,0:T(8,128)(2,1)}, u32[]{:S(2)}) copy-start(bf16[256,2048]{1,0:T(8,128)(2,1)} %q.5) | copy-start | bytes 3145732
  9.2 1.2 %copy-start.3 = (bf16[256,2048]{1,0:T(8,128)(2,1)S(1)}, bf16[256,2048]{1,0:T(8,128)(2,1)}, u32[]{:S(2)}) copy-start(bf16[256,2048]{1,0:T(8,128)(2,1)} %g.5) | copy-start | bytes 3145732
  10.4 0.7 copy-start.5
  11.1 11.3 %copy-start.14 = (s32[256]{0:T(256)S(1)}, s32[256]{0:T(256)}, u32[]{:S(2)}) copy-start(s32[256]{0:T(256)} %param.13) | copy-start | bytes 3076
  11.1 12.7 %copy-start.2 = (bf16[256,2048]{1,0:T(8,128)(2,1)S(1)}, bf16[256,2048]{1,0:T(8,128)(2,1)}, u32[]{:S(2)}) copy-start(bf16[256,2048]{1,0:T(8,128)(2,1)} %q.5) | copy-start | bytes 3145732
  11.1 12.7 %copy-start.4 = (bf16[256,2048]{1,0:T(8,128)(2,1)S(1)}, bf16[256,2048]{1,0:T(8,128)(2,1)}, u32[]{:S(2)}) copy-start(bf16[256,2048]{1,0:T(8,128)(2,1)} %g.5) | copy-start | bytes 3145732
  12.0 1.0 %copy-start.6 = (bf16[128,4096]{1,0:T(8,128)(2,1)}, bf16[128,4096]{1,0:T(8,128)(2,1)S(1)}, u32[]{:S(2)}) copy-start(bf16[128,4096]{1,0:T(8,128)(2,1)S(1)} %get-tuple-element.24.q_t) | copy-start | bytes 3145732
  13.0 1.0 copy-start.9
  18.4 12.2 %all-to-all-start = ((bf16[4,512,128]{2,1,0:T(8,128)(2,1)}), bf16[4,512,128]{2,1,0:T(8,128)(2,1)S(1)}, u32[]{:S(2)}, u32[]{:S(2)}) async-start(bf16[4,512,128]{2,1,0:T(8,128)(2,1)} %broadcast_select_fusion), calls=%async_computation | async-start | bytes 1048576 | tf_op jit(solution)/shard_map/all_to_all | solution.py:145
  23.8 1.2 %copy-start.7 = (bf16[128,4096]{1,0:T(8,128)(2,1)S(1)}, bf16[128,4096]{1,0:T(8,128)(2,1)}, u32[]{:S(2)}) copy-start(bf16[128,4096]{1,0:T(8,128)(2,1)} %copy-done.6) | copy-start | bytes 3145732
  25.0 1.2 %copy-start.10 = (bf16[128,4096]{1,0:T(8,128)(2,1)S(1)}, bf16[128,4096]{1,0:T(8,128)(2,1)}, u32[]{:S(2)}) copy-start(bf16[128,4096]{1,0:T(8,128)(2,1)} %copy-done.9) | copy-start | bytes 3145732
  29.2 1.3 %copy-start.12 = (f32[4096,128]{1,0:T(8,128)}, f32[4096,128]{1,0:T(8,128)S(1)}, u32[]{:S(2)}) copy-start(f32[4096,128]{1,0:T(8,128)S(1)} %get-tuple-element.32.dq_in) | copy-start | bytes 6291460
  30.6 1.2 %copy-start.8 = (bf16[128,4096]{1,0:T(8,128)(2,1)S(1)}, bf16[128,4096]{1,0:T(8,128)(2,1)}, u32[]{:S(2)}) copy-start(bf16[128,4096]{1,0:T(8,128)(2,1)} %copy-done.6) | copy-start | bytes 3145732
  31.8 1.2 %copy-start.11 = (bf16[128,4096]{1,0:T(8,128)(2,1)S(1)}, bf16[128,4096]{1,0:T(8,128)(2,1)}, u32[]{:S(2)}) copy-start(bf16[128,4096]{1,0:T(8,128)(2,1)} %copy-done.9) | copy-start | bytes 3145732
  33.0 1.6 %copy-start.13 = (f32[4096,128]{1,0:T(8,128)S(1)}, f32[4096,128]{1,0:T(8,128)}, u32[]{:S(2)}) copy-start(f32[4096,128]{1,0:T(8,128)} %copy-done.12) | copy-start | bytes 6291460
  36.9 18.5 %all-to-all-start.1 = ((bf16[4,512,128]{2,1,0:T(8,128)(2,1)}), bf16[4,512,128]{2,1,0:T(8,128)(2,1)S(1)}, u32[]{:S(2)}, u32[]{:S(2)}) async-start(bf16[4,512,128]{2,1,0:T(8,128)(2,1)} %get-tuple-element.36), calls=%async_computation.1 | async-start | bytes 1048576 | tf_op jit(solution)/shard_map/all_to_all | solution.py:145
  55.4 14.0 %all-to-all-start.2 = ((f32[8,1,128]{2,1,0:T(1,128)}), f32[8,1,128]{2,1,0:T(1,128)S(1)}, u32[]{:S(2)}, u32[]{:S(2)}) async-start(f32[8,1,128]{2,1,0:T(1,128)} %bitcast.3), calls=%async_computation.2 | async-start | bytes 8192 | tf_op jit(solution)/shard_map/all_to_all | solution.py:192
  63.4 31.9 %collective-permute-start.1 = (bf16[512,128]{1,0:T(8,128)(2,1)S(1)}, bf16[512,128]{1,0:T(8,128)(2,1)S(1)}, u32[]{:S(2)}, u32[]{:S(2)}) collective-permute-start(bf16[512,128]{1,0:T(8,128)(2,1)S(1)} %get-tuple-element.39), channel_id=1, source_target_pairs={{0,480},{8,488},{16,496},{24,504},{32,0},{40,8},{48,16},{56,24},{6... | collective-permute-start | bytes 393224 | tf_op jit(solution)/shard_map/ppermute | solution.py:150

commit v2 on v1

v2 whole, which is shorter than its diff:
```python
import functools
import math

import jax
import jax.numpy as jnp
from jax import lax
from jax.experimental import pallas as pl
from jax.experimental.pallas import tpu as pltpu
from jax.sharding import Mesh
from jax.sharding import PartitionSpec as P

HD = 128
ROWS = 256
HEADS = 16
REACH = 4
ROW_X = 4
LOG2E = math.log2(math.e)
SCALE = HD**-0.5
NT = (((1,), (1,)), ((), ()))
NN = (((1,), (0,)), ((), ()))
TN = (((0,), (0,)), ((), ()))
CHUNKS = 4
TAIL = 16
BF16 = jnp.bfloat16
F32 = jnp.float32


def dot(a, b, dims=NN):
    return lax.dot_general(a, b, dims, preferred_element_type=F32)


def columns(h):
    return slice(h * HD, (h + 1) * HD)


def rows_of(h):
    return slice(h * ROWS, (h + 1) * ROWS)


def pieces(x):
    first = x.astype(BF16).astype(F32)
    rest = x - first
    second = rest.astype(BF16).astype(F32)
    return first, second, (rest - second).astype(BF16).astype(F32)


def chunk_copies(source, target, sems):
    width = HEADS * HD // CHUNKS
    return [
        pltpu.make_async_copy(
            source.at[:, pl.ds(c * width, width)], target.at[:, pl.ds(c * width, width)], sems.at[c]
        )
        for c in range(CHUNKS)
    ]


def start_all(copies):
    for copy in copies:
        copy.start()


def wait_all(copies):
    for copy in copies:
        copy.wait()


def spread_kernel(own, far, slots):
    x = lax.axis_index("x")
    for i in range(ROW_X):

        @pl.when(i > x)
        def _():
            slots[i] = own[...]

        @pl.when(i <= x)
        def _():
            slots[i] = far[...]


def prepare_kernel(g_hbm, o_hbm, norm, ext, g, o, ext_t, g_sems, o_sems):
    copies = list(zip(chunk_copies(g_hbm, g, g_sems), chunk_copies(o_hbm, o, o_sems)))
    for pair in copies:
        start_all(pair)
    ones = jnp.ones((8, HD), BF16)
    place = lax.broadcasted_iota(jnp.int32, (8, ROWS), 0)
    for h in range(HEADS):
        if h % (HEADS // CHUNKS) == 0:
            wait_all(copies[h // (HEADS // CHUNKS)])
        product = g[:, columns(h)].astype(F32) * o[:, columns(h)].astype(F32)
        high = product.astype(BF16)
        low = (product - high.astype(F32)).astype(BF16)
        delta = dot(ones, high, NT) + dot(ones, low, NT)
        shift = jnp.broadcast_to(norm[h : h + 1, :] * (-(HD**0.5)), (8, ROWS))
        block = jnp.zeros((8, ROWS), F32)
        for r, term in enumerate(pieces(shift) + pieces(-delta)):
            block = jnp.where(place == r, term, block)
        ext_t[8 * h : 8 * h + 8, :] = block
    ext[...] = ext_t[...].T.astype(BF16)


def tile_grads(q, g, ext, k, v, bias, dq, dkv):
    lane = lax.broadcasted_iota(jnp.int32, (ROWS, HD), 1)
    k_wide = jnp.concatenate([k, jnp.where(lane % 8 < 3, 1.0, 0.0).astype(BF16)], axis=1)
    v_wide = jnp.concatenate([v, jnp.where((lane % 8 >= 3) & (lane % 8 < 6), 1.0, 0.0).astype(BF16)], axis=1)
    extras = [jnp.where(lane // 8 == h, ext[...], jnp.zeros((), BF16)) for h in range(HEADS)]
    q_wide = jnp.concatenate([jnp.concatenate([q[:, columns(h)], extras[h]], axis=1) for h in range(HEADS)], axis=0)
    g_wide = jnp.concatenate([jnp.concatenate([g[:, columns(h)], extras[h]], axis=1) for h in range(HEADS)], axis=0)
    scores = dot(q_wide, k_wide, NT)
    dprobs = dot(g_wide, v_wide, NT)
    probs = jnp.exp2(scores * (SCALE * LOG2E) + jnp.concatenate([bias[...]] * HEADS, axis=0))
    dscores = (probs * dprobs).astype(BF16)
    dq[...] += dot(dscores, k)
    q_rows = jnp.concatenate([q[:, columns(h)] for h in range(HEADS)], axis=0)
    g_rows = jnp.concatenate([g[:, columns(h)] for h in range(HEADS)], axis=0)
    dkv[:, :ROWS] = dot(q_rows, dscores, TN) * SCALE
    dkv[:, ROWS:] = dot(g_rows, probs.astype(BF16), TN)


def set_bias(bias, doc, ctx, offset):
    key_pos = (ctx - offset) * ROWS + lax.broadcasted_iota(jnp.int32, (ROWS, ROWS), 1)
    query_pos = ctx * ROWS + lax.broadcasted_iota(jnp.int32, (ROWS, ROWS), 0)
    start = jnp.broadcast_to(doc[...], (ROWS, ROWS)).T
    bias[...] = jnp.where((key_pos >= start) & (key_pos <= query_pos), 0.0, -1e30)


def near_kernel(first, doc, q, g, ext, own, far, dq_hbm, own_grads, far_grads, dq, bias, dkv, dq_sem):
    ctx = lax.axis_index(("z", "x"))
    dq[...] = jnp.zeros_like(dq)
    far_grads[...] = jnp.zeros_like(far_grads)
    set_bias(bias, doc, ctx, 0)
    tile_grads(q, g, ext, own[:ROWS], own[ROWS:], bias, dq, dkv)
    own_grads[:ROWS] = dkv[:, :ROWS].T
    own_grads[ROWS:] = dkv[:, ROWS:].T

    @pl.when(first[0] < (ctx - REACH + 1) * ROWS)
    def _():
        set_bias(bias, doc, ctx, REACH)
        tile_grads(q, g, ext, far[:ROWS], far[ROWS:], bias, dq, dkv)
        far_grads[:ROWS] = dkv[:, :ROWS].T.astype(BF16)
        far_grads[ROWS:] = dkv[:, ROWS:].T.astype(BF16)

    out = pltpu.make_async_copy(dq, dq_hbm, dq_sem)
    out.start()
    out.wait()


def between_kernel(
    first, doc, q, g, ext, blocks, near_hbm, far_grads, dq_hbm, parts, dq, near, total, bias, dkv, near_sem, dq_sems
):
    ctx, x = lax.axis_index(("z", "x")), lax.axis_index("x")
    near_copy = pltpu.make_async_copy(near_hbm, near, near_sem)
    near_copy.start()
    total[...] = jnp.zeros_like(total)
    parts[...] = jnp.zeros_like(parts)
    parts[x, : 2 * ROWS] = far_grads[...]
    reach = jnp.clip(lax.div(ctx * ROWS - first[0] + (ROWS - 1), ROWS), 0, REACH - 1)

    def one(offset, carry):
        slot = lax.rem(x - offset + ROW_X, ROW_X)
        set_bias(bias, doc, ctx, offset)
        tile_grads(q, g, ext, blocks[slot, :ROWS], blocks[slot, ROWS:], bias, total, dkv)
        parts[slot, :ROWS] = dkv[:, :ROWS].T.astype(BF16)
        parts[slot, ROWS : 2 * ROWS] = dkv[:, ROWS:].T.astype(BF16)
        return carry

    lax.fori_loop(1, reach + 1, one, 0)
    near_copy.wait()
    square = jnp.zeros((8, HD), F32)
    copies = chunk_copies(dq, dq_hbm, dq_sems)
    for h in range(HEADS):
        block = (total[rows_of(h), :] + near[rows_of(h), :]) * SCALE
        dq[:, columns(h)] = block.astype(BF16)
        square += jnp.sum((block * block).reshape(ROWS // 8, 8, HD), axis=0)
        if (h + 1) % (HEADS // CHUNKS) == 0:
            copies[h // (HEADS // CHUNKS)].start()
    square = jnp.broadcast_to(jnp.sum(square, axis=0, keepdims=True), (TAIL, HD))
    place = lax.broadcasted_iota(jnp.int32, (TAIL, HD), 0)
    rows = jnp.zeros((TAIL, HD), F32)
    for r, term in enumerate(pieces(square)):
        rows = jnp.where(place == r, term, rows)
    for i in range(ROW_X):
        parts[i, 2 * ROWS :] = rows.astype(BF16)
    wait_all(copies)


def rows_kernel(back, rows):
    row = jnp.sum(jnp.sum(back[:, 2 * ROWS :].astype(F32), axis=0), axis=0, keepdims=True)
    rows[...] = jnp.broadcast_to(row, rows.shape)


def fold_kernel(back, own_grads, rows, mine, onward):
    x = lax.axis_index("x")
    here, there = own_grads[...], jnp.zeros((2 * ROWS, HD), F32)
    for i in range(ROW_X):
        part = back[i, : 2 * ROWS].astype(F32)
        here += jnp.where(x < i, part, 0.0)
        there += jnp.where(x < i, 0.0, part)
    mine[...] = here
    onward[...] = there.astype(BF16)


def end_kernel(entries, squares, mine, arrived, grad_keys, grad_values, mean):
    grads = mine[...] + arrived[...].astype(F32)
    grad_keys[...] = grads[:ROWS].astype(BF16)
    grad_values[...] = grads[ROWS:].astype(BF16)
    mean[...] = jnp.sum(jnp.sum(squares[...], axis=0, keepdims=True), axis=1, keepdims=True) / entries


VMEM = pl.BlockSpec(memory_space=pltpu.VMEM)
SMEM = pl.BlockSpec(memory_space=pltpu.SMEM)
ANY = pl.BlockSpec(memory_space=pltpu.HBM)
DMA = pltpu.SemaphoreType.DMA


def call(kernel, ins, outs, scratch, args, limit=50, tiles=0.0):
    return pl.pallas_call(
        kernel,
        out_shape=tuple(jax.ShapeDtypeStruct(shape, dtype) for _, shape, dtype in outs),
        in_specs=ins,
        out_specs=tuple(space for space, _, _ in outs),
        scratch_shapes=[s if hasattr(s, "memory_space") or not isinstance(s, tuple) else pltpu.VMEM(*s) for s in scratch],
        compiler_params=pltpu.CompilerParams(vmem_limit_bytes=limit * 2**20),
        cost_estimate=pl.CostEstimate(
            flops=int(tiles * 10 * HEADS * ROWS * ROWS * HD), bytes_accessed=4 * 2**20, transcendentals=0
        ),
    )(*args)


def exchange_x(x):
    return lax.all_to_all(x, "x", 0, 0, tiled=True)


def shift_z(x, by):
    peers = lax.axis_size("z")
    return lax.ppermute(x, "z", [(i, (i + by) % peers) for i in range(peers)])


def shards(queries, keys, values, attn_out, grad_out, log_norm, doc_start):
    wide = ROWS * HEADS
    kv = (2 * ROWS, HD)
    full = ((ROWS, HEADS * HD), BF16)
    chunk_sems = DMA((CHUNKS,))

    place = lax.broadcasted_iota(jnp.int32, (2, ROWS, HD), 0)
    own = jnp.where(place == 0, keys[None], values[None]).reshape(kv)
    far = shift_z(own, 1)
    doc = doc_start.reshape(1, ROWS)
    (ext,) = call(
        prepare_kernel,
        [ANY, ANY, VMEM],
        [(VMEM, (ROWS, HD), BF16)],
        [full, full, ((HD, ROWS), F32), chunk_sems, chunk_sems],
        (grad_out, attn_out, log_norm),
        limit=53,
        tiles=1.0,
    )
    far, ext = lax.optimization_barrier((far, ext))
    (sent,) = call(spread_kernel, [VMEM, VMEM], [(VMEM, (ROW_X,) + kv, BF16)], [], (own, far), limit=2)
    blocks = exchange_x(sent)
    tile_scratch = [((ROWS, ROWS), F32), ((HD, 2 * ROWS), F32), DMA]
    dq_near, own_grads, far_grads = call(
        near_kernel,
        [SMEM, VMEM, VMEM, VMEM, VMEM, VMEM, VMEM],
        [(ANY, (wide, HD), F32), (VMEM, kv, F32), (VMEM, kv, BF16)],
        [((wide, HD), F32)] + tile_scratch,
        (doc_start, doc, queries, grad_out, ext, own, far),
        tiles=2.0,
    )
    blocks, dq_near, own_grads, far_grads = lax.optimization_barrier((blocks, dq_near, own_grads, far_grads))
    grad_queries, parts = call(
        between_kernel,
        [SMEM, VMEM, VMEM, VMEM, VMEM, VMEM, ANY, VMEM],
        [(ANY,) + full, (VMEM, (ROW_X, 2 * ROWS + TAIL, HD), BF16)],
        [full, ((wide, HD), F32), ((wide, HD), F32)] + tile_scratch + [chunk_sems],
        (doc_start, doc, queries, grad_out, ext, blocks, dq_near, far_grads),
        limit=50,
        tiles=3.0,
    )

    back = exchange_x(parts)
    members = ("z", "y", "core")
    (rows,) = call(rows_kernel, [VMEM], [(VMEM, (lax.axis_size(members), HD), F32)], [], (back,), limit=4)
    squares = lax.all_to_all(rows, members, 0, 0, tiled=True)
    mine, onward = call(
        fold_kernel, [VMEM, VMEM, VMEM], [(VMEM, kv, F32), (VMEM, kv, BF16)], [], (back, own_grads, rows), limit=4, tiles=5.0
    )
    arrived = shift_z(onward, -1)
    squares, mine = lax.optimization_barrier((squares, mine))
    entries = float(ROWS * HEADS * HD * lax.axis_size(("z", "x", "y", "core")))
    grad_keys, grad_values, mean = call(
        functools.partial(end_kernel, entries),
        [VMEM, VMEM, VMEM],
        [(VMEM, (ROWS, HD), BF16), (VMEM, (ROWS, HD), BF16), (VMEM, (1, 1), F32)],
        [],
        (squares, mine, arrived),
        limit=4,
    )
    return (grad_queries, grad_keys, grad_values, mean.reshape(()))


def solution(mesh):
    ctx, tp = ("z", "x"), ("y", "core")
    sizes = (mesh.shape["ctx"] // ROW_X, ROW_X, mesh.shape["tp"] // 2, 2)
    chips = Mesh(mesh.devices.reshape(sizes), ctx + tp)
    return jax.shard_map(
        shards,
        mesh=chips,
        in_specs=(P(ctx, tp), P(ctx, tp), P(ctx, tp), P(ctx, tp), P(ctx, tp), P(tp, ctx), P(ctx)),
        out_specs=(P(ctx, tp), P(ctx, tp), P(ctx, tp), P()),
        check_vma=False,
    )
```

time: 98 us -> 79.5 us (0.81)
  local copies, waits for them, and re-layouts: 17.2 us -> 0.82 us
  blocking collectives: 24.6 us -> 15.1 us
  waiting for transfers between devices: 10.7 us -> 19.5 us
  Pallas kernels: 6.14 us -> 13.3 us
  starting transfers between devices: 33.4 us -> 28.5 us
  between operations: 2.54 us -> 0.73 us
  other arithmetic: 2.61 us -> 1.01 us
    unnamed x31 -> x8, local copies, waits for them, and re-layouts: 15 us -> 0.73 us
    all_to_all x1, blocking collectives: 24.6 us -> 15.1 us  [exchange_x(): return lax.all_to_all(x, 'x', 0, 0, tiled=True)]
    pallas_call x3 -> x7, Pallas kernels: 6.14 us -> 13.3 us  [call(): pl.pallas_call(kernel, out_shape=tuple((jax.ShapeDtypeStruct(shape, dtype...]
    all_to_all x3 -> x2, waiting for transfers between devices: 7.15 us -> 11.8 us  [the longest x1 8.52 us: shards(): squares = lax.all_to_all(rows, members, 0, 0, tiled=True)]
    all_to_all x3 -> x2, starting transfers between devices: 23.1 us -> 18.8 us  [the longest x1 14.8 us: shards(): squares = lax.all_to_all(rows, members, 0, 0, tiled=True)]
    ppermute x2, waiting for transfers between devices: 3.53 us -> 7.73 us  [shift_z(): return lax.ppermute(x, 'z', [(i, (i + by) % peers) for i in range(peers)])]
    slice x2 -> x0, local copies, waits for them, and re-layouts: 1.17 us -> none  [the longest x1 0.66 us: shards(): return (grad_queries, grads[:ROWS], grads[ROWS:], grad_square_mean)]
  transfers between devices with their start and end apart: 5 -> 4, of which waited for: 2 -> 3; matrix products, arithmetic and copies ran while one was open for 2% -> 0% of each run, Pallas kernels for 4% -> 10%
where the time goes in v2:
time: 79.5 us; the launch traced here: 79 us
  starting transfers between devices  28.5 us (36%)
  waiting for transfers between devices  19.5 us (25%)
  blocking collectives  15.1 us (19%)
  Pallas kernels  13.3 us (17%)
  other arithmetic  1.01 us (1%)
  local copies, waits for them, and re-layouts  0.82 us (1%)
    all_to_all x1, blocking collectives, exchange_x(): return lax.all_to_all(x, 'x', 0, 0, tiled=True)  15.1 us
    all_to_all x1, starting transfers between devices, shards(): squares = lax.all_to_all(rows, members, 0, 0, tiled=True)  14.8 us
    pallas_call x7, Pallas kernels, call(): pl.pallas_call(kernel, out_shape=tuple((jax.ShapeDtypeStruct(shape, dtype...  13.3 us
    ppermute x2, starting transfers between devices, shift_z(): return lax.ppermute(x, 'z', [(i, (i + by) % peers) for i in range(peers)])  9.71 us
    all_to_all x1, waiting for transfers between devices, shards(): squares = lax.all_to_all(rows, members, 0, 0, tiled=True)  8.52 us
    ppermute x2, waiting for transfers between devices, shift_z(): return lax.ppermute(x, 'z', [(i, (i + by) % peers) for i in range(peers)])  7.73 us
    all_to_all x1, starting transfers between devices, exchange_x(): return lax.all_to_all(x, 'x', 0, 0, tiled=True)  4.01 us
    all_to_all x1, waiting for transfers between devices, exchange_x(): return lax.all_to_all(x, 'x', 0, 0, tiled=True)  3.25 us
  transfers between devices with their start and end apart: 4, of which 3 were waited for; matrix products, arithmetic and copies ran while one was open for 0% of the time, Pallas kernels for 10%

profile of v2, /device:TPU:1, one launch (start us, length us, event | category | flops | bytes accessed | tf_op | source)
XLA Modules:
  0.0 79.0 jit_solution(16010773567556195969)
XLA Ops:
  0.6 0.1 iota.11
  0.7 1.0 %bitcast_select_fusion.own = bf16[512,128]{1,0:T(8,128)(2,1)S(1)} fusion(pred[512]{0:T(512)(128)(4,1)S(1)} %iota.12, bf16[256,128]{1,0:T(8,128)(2,1)} %param.9, bf16[256,128]{1,0:T(8,128)(2,1)} %param.8), kind=kLoop, calls=%fused_computation | loop fusion | flops 65536 | bytes 262656 | tf_op jit(solution)/shard_map/jit(_where)/select_n | solution.py:245
  1.7 0.0 copy-start
  1.8 0.0 copy-start.1
  1.8 4.5 %collective-permute-start = (bf16[512,128]{1,0:T(8,128)(2,1)S(1)}, bf16[512,128]{1,0:T(8,128)(2,1)S(1)}, u32[]{:S(2)}, u32[]{:S(2)}) collective-permute-start(bf16[512,128]{1,0:T(8,128)(2,1)S(1)} %bitcast_select_fusion.own), channel_id=1, source_target_pairs={{0,32},{32,64},{64,96},{96,128},{128,160},{160,192},{192,224},{224... | collective-permute-start | bytes 393224 | tf_op jit(solution)/shard_map/ppermute | solution.py:235
  6.3 0.0 copy-start.2
  6.3 0.7 copy-done.2
  7.0 0.0 copy-start.3
  7.0 2.3 %shard_map.102.ext = bf16[256,128]{1,0:T(8,128)(2,1)S(1)} custom-call(bf16[256,2048]{1,0:T(8,128)(2,1)} %g.3, bf16[256,2048]{1,0:T(8,128)(2,1)} %o_hbm.1, f32[16,256]{1,0:T(8,128)S(1)} %copy-done.2), custom_call_target="tpu_custom_call" | custom-call | flops 1342177280 | bytes 4194304 | tf_op jit(solution)/shard_map/pallas_call | solution.py:216
  9.3 7.7 %collective-permute-done.far = bf16[512,128]{1,0:T(8,128)(2,1)S(1)} collective-permute-done((bf16[512,128]{1,0:T(8,128)(2,1)S(1)}, bf16[512,128]{1,0:T(8,128)(2,1)S(1)}, u32[]{:S(2)}, u32[]{:S(2)}) %collective-permute-start) | collective-permute-done | bytes 131104 | tf_op jit(solution)/shard_map/ppermute | solution.py:235
  17.1 0.8 %shard_map.103 = bf16[4,512,128]{2,1,0:T(8,128)(2,1)} custom-call(bf16[512,128]{1,0:T(8,128)(2,1)S(1)} %bitcast_select_fusion.own, bf16[512,128]{1,0:T(8,128)(2,1)S(1)} %collective-permute-done.far), custom_call_target="tpu_custom_call" | custom-call | bytes 4194304 | tf_op jit(solution)/shard_map/pallas_call | solution.py:216
  17.9 4.0 %all-to-all-start = ((bf16[4,512,128]{2,1,0:T(8,128)(2,1)}), bf16[4,512,128]{2,1,0:T(8,128)(2,1)S(1)}, u32[]{:S(2)}, u32[]{:S(2)}) async-start(bf16[4,512,128]{2,1,0:T(8,128)(2,1)} %shard_map.103), calls=%async_computation | async-start | bytes 1048576 | tf_op jit(solution)/shard_map/all_to_all | solution.py:230
  21.9 0.0 copy-done
  21.9 0.0 copy-done.1
  21.9 0.0 copy-done.3
  21.9 4.4 %shard_map.104 = (f32[4096,128]{1,0:T(8,128)}, f32[512,128]{1,0:T(8,128)S(1)}, bf16[512,128]{1,0:T(8,128)(2,1)S(1)}) custom-call(s32[256]{0:T(256)S(1)} %copy-done.3, s32[1,256]{1,0:T(1,128)S(1)} %bitcast.11, bf16[256,2048]{1,0:T(8,128)(2,1)S(1)} %copy-done, bf16[256,2048]{1,0:T(8,128)(2,1)S(1)} %copy-done.1, bf16[256,128]{1,0:T(8,128)(2,1)S(1)} %shard_map.102.ext, ...), custom_call_target="tpu_custom_call" | custom-call | flops 2684354560 | bytes 4194304 | tf_op jit(solution)/shard_map/pallas_call | solution.py:216
  26.4 3.2 %all-to-all-done.blocks = bf16[4,512,128]{2,1,0:T(8,128)(2,1)S(1)} async-done(((bf16[4,512,128]{2,1,0:T(8,128)(2,1)}), bf16[4,512,128]{2,1,0:T(8,128)(2,1)S(1)}, u32[]{:S(2)}, u32[]{:S(2)}) %all-to-all-start) | async-done | bytes 524320 | tf_op jit(solution)/shard_map/all_to_all | solution.py:230
  29.6 3.2 %shard_map.105 = (bf16[256,2048]{1,0:T(8,128)(2,1)}, bf16[4,528,128]{2,1,0:T(8,128)(2,1)S(1)}) custom-call(s32[256]{0:T(256)S(1)} %copy-done.3, s32[1,256]{1,0:T(1,128)S(1)} %bitcast.12, bf16[256,2048]{1,0:T(8,128)(2,1)S(1)} %copy-done, bf16[256,2048]{1,0:T(8,128)(2,1)S(1)} %copy-done.1, bf16[256,128]{1,0:T(8,128)(2,1)S(1)} %shard_map.102.ext, ...), custom_call_target="tpu_custom_call" | custom-call | flops 4026531840 | bytes 4194304 | tf_op jit(solution)/shard_map/pallas_call | solution.py:216
  32.9 15.1 %all_to_all.22.back = bf16[4,528,128]{2,1,0:T(8,128)(2,1)S(1)} all-to-all(bf16[4,528,128]{2,1,0:T(8,128)(2,1)S(1)} %get-tuple-element.31), channel_id=1, replica_groups=mesh['z'=16,'x'=4,'y'=4,'core'=2] {'x'}, dimensions={0} | all-to-all | bytes 1081344 | tf_op jit(solution)/shard_map/all_to_all | solution.py:230
  48.0 0.6 shard_map.106.rows
  48.6 14.8 %all-to-all-start.2 = ((f32[128,1,128]{2,1,0:T(1,128)}), f32[128,1,128]{2,1,0:T(1,128)S(1)}, u32[]{:S(2)}, u32[]{:S(2)}) async-start(f32[128,1,128]{2,1,0:T(1,128)} %bitcast.4), calls=%async_computation.2 | async-start | bytes 131072 | tf_op jit(solution)/shard_map/all_to_all | solution.py:283
  63.4 1.1 %shard_map.107 = (f32[512,128]{1,0:T(8,128)S(1)}, bf16[512,128]{1,0:T(8,128)(2,1)S(1)}) custom-call(bf16[4,528,128]{2,1,0:T(8,128)(2,1)S(1)} %all_to_all.22.back, f32[512,128]{1,0:T(8,128)S(1)} %get-tuple-element.32.own_grads, f32[128,128]{1,0:T(8,128)} %shard_map.106.rows), custom_call_target="tpu_custom_call" | custom-call | flops 6710886400 | bytes 4194304 | tf_op jit(solution)/shard_map/pallas_call | solution.py:216
  64.5 5.2 %collective-permute-start.1 = (bf16[512,128]{1,0:T(8,128)(2,1)S(1)}, bf16[512,128]{1,0:T(8,128)(2,1)S(1)}, u32[]{:S(2)}, u32[]{:S(2)}) collective-permute-start(bf16[512,128]{1,0:T(8,128)(2,1)S(1)} %get-tuple-element.36), channel_id=1, source_target_pairs={{0,480},{32,0},{64,32},{96,64},{128,96},{160,128},{192,160},{224,1... | collective-permute-start | bytes 393224 | tf_op jit(solution)/shard_map/ppermute | solution.py:235
  69.7 8.5 %all-to-all-done.2 = f32[128,1,128]{2,1,0:T(1,128)S(1)} async-done(((f32[128,1,128]{2,1,0:T(1,128)}), f32[128,1,128]{2,1,0:T(1,128)S(1)}, u32[]{:S(2)}, u32[]{:S(2)}) %all-to-all-start.2) | async-done | bytes 65568 | tf_op jit(solution)/shard_map/all_to_all | solution.py:283
  78.3 0.0 collective-permute-done.1.arrived
  78.3 0.7 shard_map.108
  (2 shorter events, 0.0 us)
Async XLA Ops:
  1.7 20.2 %copy-start = (bf16[256,2048]{1,0:T(8,128)(2,1)S(1)}, bf16[256,2048]{1,0:T(8,128)(2,1)}, u32[]{:S(2)}) copy-start(bf16[256,2048]{1,0:T(8,128)(2,1)} %q.3) | copy-start | bytes 3145732
  1.8 20.2 %copy-start.1 = (bf16[256,2048]{1,0:T(8,128)(2,1)S(1)}, bf16[256,2048]{1,0:T(8,128)(2,1)}, u32[]{:S(2)}) copy-start(bf16[256,2048]{1,0:T(8,128)(2,1)} %g.3) | copy-start | bytes 3145732
  1.8 15.3 %collective-permute-start = (bf16[512,128]{1,0:T(8,128)(2,1)S(1)}, bf16[512,128]{1,0:T(8,128)(2,1)S(1)}, u32[]{:S(2)}, u32[]{:S(2)}) collective-permute-start(bf16[512,128]{1,0:T(8,128)(2,1)S(1)} %bitcast_select_fusion.own), channel_id=1, source_target_pairs={{0,32},{32,64},{64,96},{96,128},{128,160},{160,192},{192,224},{224... | collective-permute-start | bytes 393224 | tf_op jit(solution)/shard_map/ppermute | solution.py:235
  6.3 0.7 copy-start.2
  7.0 14.9 %copy-start.3 = (s32[256]{0:T(256)S(1)}, s32[256]{0:T(256)}, u32[]{:S(2)}) copy-start(s32[256]{0:T(256)} %first.3) | copy-start | bytes 3076
  17.9 11.7 %all-to-all-start = ((bf16[4,512,128]{2,1,0:T(8,128)(2,1)}), bf16[4,512,128]{2,1,0:T(8,128)(2,1)S(1)}, u32[]{:S(2)}, u32[]{:S(2)}) async-start(bf16[4,512,128]{2,1,0:T(8,128)(2,1)} %shard_map.103), calls=%async_computation | async-start | bytes 1048576 | tf_op jit(solution)/shard_map/all_to_all | solution.py:230
  48.6 29.6 %all-to-all-start.2 = ((f32[128,1,128]{2,1,0:T(1,128)}), f32[128,1,128]{2,1,0:T(1,128)S(1)}, u32[]{:S(2)}, u32[]{:S(2)}) async-start(f32[128,1,128]{2,1,0:T(1,128)} %bitcast.4), calls=%async_computation.2 | async-start | bytes 131072 | tf_op jit(solution)/shard_map/all_to_all | solution.py:283
  64.5 13.7 %collective-permute-start.1 = (bf16[512,128]{1,0:T(8,128)(2,1)S(1)}, bf16[512,128]{1,0:T(8,128)(2,1)S(1)}, u32[]{:S(2)}, u32[]{:S(2)}) collective-permute-start(bf16[512,128]{1,0:T(8,128)(2,1)S(1)} %get-tuple-element.36), channel_id=1, source_target_pairs={{0,480},{32,0},{64,32},{96,64},{128,96},{160,128},{192,160},{224,1... | collective-permute-start | bytes 393224 | tf_op jit(solution)/shard_map/ppermute | solution.py:235

commit v3 on v2

--- a/solution.py
+++ b/solution.py
@@ -165,14 +165,17 @@
 
     lax.fori_loop(1, reach + 1, one, 0)
     near_copy.wait()
-    square = jnp.zeros((8, HD), F32)
     copies = chunk_copies(dq, dq_hbm, dq_sems)
     for h in range(HEADS):
         block = (total[rows_of(h), :] + near[rows_of(h), :]) * SCALE
+        total[rows_of(h), :] = block
         dq[:, columns(h)] = block.astype(BF16)
-        square += jnp.sum((block * block).reshape(ROWS // 8, 8, HD), axis=0)
         if (h + 1) % (HEADS // CHUNKS) == 0:
             copies[h // (HEADS // CHUNKS)].start()
+    square = jnp.zeros((8, HD), F32)
+    for h in range(HEADS):
+        block = total[rows_of(h), :]
+        square += jnp.sum((block * block).reshape(ROWS // 8, 8, HD), axis=0)
     square = jnp.broadcast_to(jnp.sum(square, axis=0, keepdims=True), (TAIL, HD))
     place = lax.broadcasted_iota(jnp.int32, (TAIL, HD), 0)
     rows = jnp.zeros((TAIL, HD), F32)
@@ -183,13 +186,10 @@
     wait_all(copies)
 
 
-def rows_kernel(back, rows):
+def fold_kernel(back, own_grads, rows, mine, onward):
+    x = lax.axis_index("x")
     row = jnp.sum(jnp.sum(back[:, 2 * ROWS :].astype(F32), axis=0), axis=0, keepdims=True)
     rows[...] = jnp.broadcast_to(row, rows.shape)
-
-
-def fold_kernel(back, own_grads, rows, mine, onward):
-    x = lax.axis_index("x")
     here, there = own_grads[...], jnp.zeros((2 * ROWS, HD), F32)
     for i in range(ROW_X):
         part = back[i, : 2 * ROWS].astype(F32)
@@ -273,19 +273,21 @@
         [(ANY,) + full, (VMEM, (ROW_X, 2 * ROWS + TAIL, HD), BF16)],
         [full, ((wide, HD), F32), ((wide, HD), F32)] + tile_scratch + [chunk_sems],
         (doc_start, doc, queries, grad_out, ext, blocks, dq_near, far_grads),
-        limit=50,
         tiles=3.0,
     )
 
     back = exchange_x(parts)
     members = ("z", "y", "core")
-    (rows,) = call(rows_kernel, [VMEM], [(VMEM, (lax.axis_size(members), HD), F32)], [], (back,), limit=4)
+    rows, mine, onward = call(
+        fold_kernel,
+        [VMEM, VMEM],
+        [(VMEM, (lax.axis_size(members), HD), F32), (VMEM, kv, F32), (VMEM, kv, BF16)],
+        [],
+        (back, own_grads),
+        limit=4,
+    )
     squares = lax.all_to_all(rows, members, 0, 0, tiled=True)
-    mine, onward = call(
-        fold_kernel, [VMEM, VMEM, VMEM], [(VMEM, kv, F32), (VMEM, kv, BF16)], [], (back, own_grads, rows), limit=4, tiles=5.0
-    )
     arrived = shift_z(onward, -1)
-    squares, mine = lax.optimization_barrier((squares, mine))
     entries = float(ROWS * HEADS * HD * lax.axis_size(("z", "x", "y", "core")))
     grad_keys, grad_values, mean = call(
         functools.partial(end_kernel, entries),

time: 79.5 us -> 78.7 us (0.990)
  waiting for transfers between devices: 19.5 us -> 20.6 us
  Pallas kernels: 13.3 us -> 12.4 us
  starting transfers between devices: 28.5 us -> 27.7 us
    ppermute x2, waiting for transfers between devices: 7.73 us -> 10.8 us  [shift_z(): return lax.ppermute(x, 'z', [(i, (i + by) % peers) for i in range(peers)])]
    all_to_all x1, waiting for transfers between devices: 8.52 us -> 6.55 us  [shards(): squares = lax.all_to_all(rows, members, 0, 0, tiled=True)]
    pallas_call x7 -> x6, Pallas kernels: 13.3 us -> 12.4 us  [call(): pl.pallas_call(kernel, out_shape=tuple((jax.ShapeDtypeStruct(shape, dtype...]
    all_to_all x1, starting transfers between devices: 14.8 us -> 14 us  [shards(): squares = lax.all_to_all(rows, members, 0, 0, tiled=True)]
  transfers between devices with their start and end apart: 4 -> 4, of which waited for: 3 -> 4; matrix products, arithmetic and copies ran while one was open for 0% -> 0% of each run, Pallas kernels for 10% -> 9%
where the time goes in v3:
time: 78.7 us; the launch traced here: 78.3 us
  starting transfers between devices  27.7 us (35%)
  waiting for transfers between devices  20.6 us (26%)
  blocking collectives  15.1 us (19%)
  Pallas kernels  12.4 us (16%)
  other arithmetic  1.01 us (1%)
  local copies, waits for them, and re-layouts  0.82 us (1%)
    all_to_all x1, blocking collectives, exchange_x(): return lax.all_to_all(x, 'x', 0, 0, tiled=True)  15.1 us
    all_to_all x1, starting transfers between devices, shards(): squares = lax.all_to_all(rows, members, 0, 0, tiled=True)  14 us
    pallas_call x6, Pallas kernels, call(): pl.pallas_call(kernel, out_shape=tuple((jax.ShapeDtypeStruct(shape, dtype...  12.4 us
    ppermute x2, waiting for transfers between devices, shift_z(): return lax.ppermute(x, 'z', [(i, (i + by) % peers) for i in range(peers)])  10.8 us
    ppermute x2, starting transfers between devices, shift_z(): return lax.ppermute(x, 'z', [(i, (i + by) % peers) for i in range(peers)])  9.71 us
    all_to_all x1, waiting for transfers between devices, shards(): squares = lax.all_to_all(rows, members, 0, 0, tiled=True)  6.55 us
    all_to_all x1, starting transfers between devices, exchange_x(): return lax.all_to_all(x, 'x', 0, 0, tiled=True)  4.01 us
    all_to_all x1, waiting for transfers between devices, exchange_x(): return lax.all_to_all(x, 'x', 0, 0, tiled=True)  3.25 us
  transfers between devices with their start and end apart: 4, of which 4 were waited for; matrix products, arithmetic and copies ran while one was open for 0% of the time, Pallas kernels for 9%

profile of v3, /device:TPU:1, one launch (start us, length us, event | category | flops | bytes accessed | tf_op | source)
XLA Modules:
  0.0 78.3 jit_solution(10231887350295456958)
XLA Ops:
  0.6 0.1 iota.11
  0.7 1.0 %bitcast_select_fusion.own = bf16[512,128]{1,0:T(8,128)(2,1)S(1)} fusion(pred[512]{0:T(512)(128)(4,1)S(1)} %iota.12, bf16[256,128]{1,0:T(8,128)(2,1)} %param.9, bf16[256,128]{1,0:T(8,128)(2,1)} %param.8), kind=kLoop, calls=%fused_computation | loop fusion | flops 65536 | bytes 262656 | tf_op jit(solution)/shard_map/jit(_where)/select_n | solution.py:245
  1.7 0.0 copy-start
  1.8 0.0 copy-start.1
  1.8 4.5 %collective-permute-start = (bf16[512,128]{1,0:T(8,128)(2,1)S(1)}, bf16[512,128]{1,0:T(8,128)(2,1)S(1)}, u32[]{:S(2)}, u32[]{:S(2)}) collective-permute-start(bf16[512,128]{1,0:T(8,128)(2,1)S(1)} %bitcast_select_fusion.own), channel_id=1, source_target_pairs={{0,32},{32,64},{64,96},{96,128},{128,160},{160,192},{192,224},{224... | collective-permute-start | bytes 393224 | tf_op jit(solution)/shard_map/ppermute | solution.py:235
  6.3 0.0 copy-start.2
  6.3 0.7 copy-done.2
  7.0 0.0 copy-start.3
  7.0 2.3 %shard_map.102.ext = bf16[256,128]{1,0:T(8,128)(2,1)S(1)} custom-call(bf16[256,2048]{1,0:T(8,128)(2,1)} %g.3, bf16[256,2048]{1,0:T(8,128)(2,1)} %o_hbm.1, f32[16,256]{1,0:T(8,128)S(1)} %copy-done.2), custom_call_target="tpu_custom_call" | custom-call | flops 1342177280 | bytes 4194304 | tf_op jit(solution)/shard_map/pallas_call | solution.py:216
  9.3 7.7 %collective-permute-done.far = bf16[512,128]{1,0:T(8,128)(2,1)S(1)} collective-permute-done((bf16[512,128]{1,0:T(8,128)(2,1)S(1)}, bf16[512,128]{1,0:T(8,128)(2,1)S(1)}, u32[]{:S(2)}, u32[]{:S(2)}) %collective-permute-start) | collective-permute-done | bytes 131104 | tf_op jit(solution)/shard_map/ppermute | solution.py:235
  17.1 0.8 %shard_map.103 = bf16[4,512,128]{2,1,0:T(8,128)(2,1)} custom-call(bf16[512,128]{1,0:T(8,128)(2,1)S(1)} %bitcast_select_fusion.own, bf16[512,128]{1,0:T(8,128)(2,1)S(1)} %collective-permute-done.far), custom_call_target="tpu_custom_call" | custom-call | bytes 4194304 | tf_op jit(solution)/shard_map/pallas_call | solution.py:216
  17.9 4.0 %all-to-all-start = ((bf16[4,512,128]{2,1,0:T(8,128)(2,1)}), bf16[4,512,128]{2,1,0:T(8,128)(2,1)S(1)}, u32[]{:S(2)}, u32[]{:S(2)}) async-start(bf16[4,512,128]{2,1,0:T(8,128)(2,1)} %shard_map.103), calls=%async_computation | async-start | bytes 1048576 | tf_op jit(solution)/shard_map/all_to_all | solution.py:230
  21.9 0.0 copy-done
  21.9 0.0 copy-done.1
  21.9 0.0 copy-done.3
  21.9 4.4 %shard_map.104 = (f32[4096,128]{1,0:T(8,128)}, f32[512,128]{1,0:T(8,128)S(1)}, bf16[512,128]{1,0:T(8,128)(2,1)S(1)}) custom-call(s32[256]{0:T(256)S(1)} %copy-done.3, s32[1,256]{1,0:T(1,128)S(1)} %bitcast.11, bf16[256,2048]{1,0:T(8,128)(2,1)S(1)} %copy-done, bf16[256,2048]{1,0:T(8,128)(2,1)S(1)} %copy-done.1, bf16[256,128]{1,0:T(8,128)(2,1)S(1)} %shard_map.102.ext, ...), custom_call_target="tpu_custom_call" | custom-call | flops 2684354560 | bytes 4194304 | tf_op jit(solution)/shard_map/pallas_call | solution.py:216
  26.4 3.2 %all-to-all-done.blocks = bf16[4,512,128]{2,1,0:T(8,128)(2,1)S(1)} async-done(((bf16[4,512,128]{2,1,0:T(8,128)(2,1)}), bf16[4,512,128]{2,1,0:T(8,128)(2,1)S(1)}, u32[]{:S(2)}, u32[]{:S(2)}) %all-to-all-start) | async-done | bytes 524320 | tf_op jit(solution)/shard_map/all_to_all | solution.py:230
  29.6 3.3 %shard_map.105 = (bf16[256,2048]{1,0:T(8,128)(2,1)}, bf16[4,528,128]{2,1,0:T(8,128)(2,1)S(1)}) custom-call(s32[256]{0:T(256)S(1)} %copy-done.3, s32[1,256]{1,0:T(1,128)S(1)} %bitcast.12, bf16[256,2048]{1,0:T(8,128)(2,1)S(1)} %copy-done, bf16[256,2048]{1,0:T(8,128)(2,1)S(1)} %copy-done.1, bf16[256,128]{1,0:T(8,128)(2,1)S(1)} %shard_map.102.ext, ...), custom_call_target="tpu_custom_call" | custom-call | flops 4026531840 | bytes 4194304 | tf_op jit(solution)/shard_map/pallas_call | solution.py:216
  33.0 15.1 %all_to_all.21.back = bf16[4,528,128]{2,1,0:T(8,128)(2,1)S(1)} all-to-all(bf16[4,528,128]{2,1,0:T(8,128)(2,1)S(1)} %get-tuple-element.30), channel_id=1, replica_groups=mesh['z'=16,'x'=4,'y'=4,'core'=2] {'x'}, dimensions={0} | all-to-all | bytes 1081344 | tf_op jit(solution)/shard_map/all_to_all | solution.py:230
  48.0 0.7 shard_map.106
  48.8 14.0 %all-to-all-start.2 = ((f32[128,1,128]{2,1,0:T(1,128)}), f32[128,1,128]{2,1,0:T(1,128)S(1)}, u32[]{:S(2)}, u32[]{:S(2)}) async-start(f32[128,1,128]{2,1,0:T(1,128)} %bitcast.4), calls=%async_computation.2 | async-start | bytes 131072 | tf_op jit(solution)/shard_map/all_to_all | solution.py:289
  62.8 5.2 %collective-permute-start.1 = (bf16[512,128]{1,0:T(8,128)(2,1)S(1)}, bf16[512,128]{1,0:T(8,128)(2,1)S(1)}, u32[]{:S(2)}, u32[]{:S(2)}) collective-permute-start(bf16[512,128]{1,0:T(8,128)(2,1)S(1)} %get-tuple-element.34), channel_id=1, source_target_pairs={{0,480},{32,0},{64,32},{96,64},{128,96},{160,128},{192,160},{224,1... | collective-permute-start | bytes 393224 | tf_op jit(solution)/shard_map/ppermute | solution.py:235
  68.0 3.1 %collective-permute-done.1.arrived = bf16[512,128]{1,0:T(8,128)(2,1)S(1)} collective-permute-done((bf16[512,128]{1,0:T(8,128)(2,1)S(1)}, bf16[512,128]{1,0:T(8,128)(2,1)S(1)}, u32[]{:S(2)}, u32[]{:S(2)}) %collective-permute-start.1) | collective-permute-done | bytes 131104 | tf_op jit(solution)/shard_map/ppermute | solution.py:235
  71.1 6.5 %all-to-all-done.2 = f32[128,1,128]{2,1,0:T(1,128)S(1)} async-done(((f32[128,1,128]{2,1,0:T(1,128)}), f32[128,1,128]{2,1,0:T(1,128)S(1)}, u32[]{:S(2)}, u32[]{:S(2)}) %all-to-all-start.2) | async-done | bytes 65568 | tf_op jit(solution)/shard_map/all_to_all | solution.py:289
  77.6 0.7 shard_map.107
  (2 shorter events, 0.0 us)
Async XLA Ops:
  1.7 20.2 %copy-start = (bf16[256,2048]{1,0:T(8,128)(2,1)S(1)}, bf16[256,2048]{1,0:T(8,128)(2,1)}, u32[]{:S(2)}) copy-start(bf16[256,2048]{1,0:T(8,128)(2,1)} %q.3) | copy-start | bytes 3145732
  1.8 20.2 %copy-start.1 = (bf16[256,2048]{1,0:T(8,128)(2,1)S(1)}, bf16[256,2048]{1,0:T(8,128)(2,1)}, u32[]{:S(2)}) copy-start(bf16[256,2048]{1,0:T(8,128)(2,1)} %g.3) | copy-start | bytes 3145732
  1.8 15.3 %collective-permute-start = (bf16[512,128]{1,0:T(8,128)(2,1)S(1)}, bf16[512,128]{1,0:T(8,128)(2,1)S(1)}, u32[]{:S(2)}, u32[]{:S(2)}) collective-permute-start(bf16[512,128]{1,0:T(8,128)(2,1)S(1)} %bitcast_select_fusion.own), channel_id=1, source_target_pairs={{0,32},{32,64},{64,96},{96,128},{128,160},{160,192},{192,224},{224... | collective-permute-start | bytes 393224 | tf_op jit(solution)/shard_map/ppermute | solution.py:235
  6.3 0.7 copy-start.2
  7.0 14.9 %copy-start.3 = (s32[256]{0:T(256)S(1)}, s32[256]{0:T(256)}, u32[]{:S(2)}) copy-start(s32[256]{0:T(256)} %first.3) | copy-start | bytes 3076
  17.9 11.7 %all-to-all-start = ((bf16[4,512,128]{2,1,0:T(8,128)(2,1)}), bf16[4,512,128]{2,1,0:T(8,128)(2,1)S(1)}, u32[]{:S(2)}, u32[]{:S(2)}) async-start(bf16[4,512,128]{2,1,0:T(8,128)(2,1)} %shard_map.103), calls=%async_computation | async-start | bytes 1048576 | tf_op jit(solution)/shard_map/all_to_all | solution.py:230
  48.8 28.8 %all-to-all-start.2 = ((f32[128,1,128]{2,1,0:T(1,128)}), f32[128,1,128]{2,1,0:T(1,128)S(1)}, u32[]{:S(2)}, u32[]{:S(2)}) async-start(f32[128,1,128]{2,1,0:T(1,128)} %bitcast.4), calls=%async_computation.2 | async-start | bytes 131072 | tf_op jit(solution)/shard_map/all_to_all | solution.py:289
  62.8 8.3 %collective-permute-start.1 = (bf16[512,128]{1,0:T(8,128)(2,1)S(1)}, bf16[512,128]{1,0:T(8,128)(2,1)S(1)}, u32[]{:S(2)}, u32[]{:S(2)}) collective-permute-start(bf16[512,128]{1,0:T(8,128)(2,1)S(1)} %get-tuple-element.34), channel_id=1, source_target_pairs={{0,480},{32,0},{64,32},{96,64},{128,96},{160,128},{192,160},{224,1... | collective-permute-start | bytes 393224 | tf_op jit(solution)/shard_map/ppermute | solution.py:235

commit v4 on v2

--- a/solution.py
+++ b/solution.py
@@ -165,14 +165,17 @@
 
     lax.fori_loop(1, reach + 1, one, 0)
     near_copy.wait()
-    square = jnp.zeros((8, HD), F32)
     copies = chunk_copies(dq, dq_hbm, dq_sems)
     for h in range(HEADS):
         block = (total[rows_of(h), :] + near[rows_of(h), :]) * SCALE
+        total[rows_of(h), :] = block
         dq[:, columns(h)] = block.astype(BF16)
-        square += jnp.sum((block * block).reshape(ROWS // 8, 8, HD), axis=0)
         if (h + 1) % (HEADS // CHUNKS) == 0:
             copies[h // (HEADS // CHUNKS)].start()
+    square = jnp.zeros((8, HD), F32)
+    for h in range(HEADS):
+        block = total[rows_of(h), :]
+        square += jnp.sum((block * block).reshape(ROWS // 8, 8, HD), axis=0)
     square = jnp.broadcast_to(jnp.sum(square, axis=0, keepdims=True), (TAIL, HD))
     place = lax.broadcasted_iota(jnp.int32, (TAIL, HD), 0)
     rows = jnp.zeros((TAIL, HD), F32)
@@ -186,6 +189,10 @@
 def rows_kernel(back, rows):
     row = jnp.sum(jnp.sum(back[:, 2 * ROWS :].astype(F32), axis=0), axis=0, keepdims=True)
     rows[...] = jnp.broadcast_to(row, rows.shape)
+
+
+def sum_kernel(summed, rows):
+    rows[...] = jnp.broadcast_to(jnp.sum(summed[...], axis=0, keepdims=True), rows.shape)
 
 
 def fold_kernel(back, own_grads, rows, mine, onward):
@@ -273,19 +280,19 @@
         [(ANY,) + full, (VMEM, (ROW_X, 2 * ROWS + TAIL, HD), BF16)],
         [full, ((wide, HD), F32), ((wide, HD), F32)] + tile_scratch + [chunk_sems],
         (doc_start, doc, queries, grad_out, ext, blocks, dq_near, far_grads),
-        limit=50,
         tiles=3.0,
     )
 
     back = exchange_x(parts)
-    members = ("z", "y", "core")
-    (rows,) = call(rows_kernel, [VMEM], [(VMEM, (lax.axis_size(members), HD), F32)], [], (back,), limit=4)
-    squares = lax.all_to_all(rows, members, 0, 0, tiled=True)
+    chip, ring = ("y", "core"), lax.axis_size("z")
+    (rows,) = call(rows_kernel, [VMEM], [(VMEM, (lax.axis_size(chip), HD), F32)], [], (back,), limit=4)
+    summed = lax.all_to_all(rows, chip, 0, 0, tiled=True)
     mine, onward = call(
-        fold_kernel, [VMEM, VMEM, VMEM], [(VMEM, kv, F32), (VMEM, kv, BF16)], [], (back, own_grads, rows), limit=4, tiles=5.0
+        fold_kernel, [VMEM] * 3, [(VMEM, kv, F32), (VMEM, kv, BF16)], [], (back, own_grads, rows), limit=4, tiles=5.0
     )
     arrived = shift_z(onward, -1)
-    squares, mine = lax.optimization_barrier((squares, mine))
+    (rows,) = call(sum_kernel, [VMEM], [(VMEM, (ring, HD), F32)], [], (summed,), limit=4, tiles=40.0)
+    squares = lax.all_to_all(rows, "z", 0, 0, tiled=True)
     entries = float(ROWS * HEADS * HD * lax.axis_size(("z", "x", "y", "core")))
     grad_keys, grad_values, mean = call(
         functools.partial(end_kernel, entries),

time: 79.5 us -> 82.9 us (1.043)
  blocking collectives: 15.1 us -> 35 us
  starting transfers between devices: 28.5 us -> 19.6 us
  waiting for transfers between devices: 19.5 us -> 12.1 us
    all_to_all x0 -> x1, blocking collectives: none -> 19.9 us  [shards(): squares = lax.all_to_all(rows, 'z', 0, 0, tiled=True)]
    all_to_all x1, waiting for transfers between devices: 8.52 us -> 1.11 us  [shards(): summed = lax.all_to_all(rows, chip, 0, 0, tiled=True)]
    all_to_all x1, starting transfers between devices: 14.8 us -> 8.62 us  [shards(): summed = lax.all_to_all(rows, chip, 0, 0, tiled=True)]
    ppermute x2, starting transfers between devices: 9.71 us -> 6.95 us  [shift_z(): return lax.ppermute(x, 'z', [(i, (i + by) % peers) for i in range(peers)])]
    pallas_call x7 -> x8, Pallas kernels: 13.3 us -> 13.2 us  [call(): pl.pallas_call(kernel, out_shape=tuple((jax.ShapeDtypeStruct(shape, dtype...]
  transfers between devices with their start and end apart: 4 -> 4, of which waited for: 3 -> 3; matrix products, arithmetic and copies ran while one was open for 0% -> 0% of each run, Pallas kernels for 10% -> 9%
where the time goes in v4:
time: 82.9 us; the launch traced here: 82.4 us
  blocking collectives  35 us (42%)
  starting transfers between devices  19.6 us (24%)
  Pallas kernels  13.2 us (16%)
  waiting for transfers between devices  12.1 us (15%)
  other arithmetic  1.01 us (1%)
    all_to_all x1, blocking collectives, shards(): squares = lax.all_to_all(rows, 'z', 0, 0, tiled=True)  19.9 us
    all_to_all x1, blocking collectives, exchange_x(): return lax.all_to_all(x, 'x', 0, 0, tiled=True)  15.1 us
    pallas_call x8, Pallas kernels, call(): pl.pallas_call(kernel, out_shape=tuple((jax.ShapeDtypeStruct(shape, dtype...  13.2 us
    all_to_all x1, starting transfers between devices, shards(): summed = lax.all_to_all(rows, chip, 0, 0, tiled=True)  8.62 us
    ppermute x2, waiting for transfers between devices, shift_z(): return lax.ppermute(x, 'z', [(i, (i + by) % peers) for i in range(peers)])  7.73 us
    ppermute x2, starting transfers between devices, shift_z(): return lax.ppermute(x, 'z', [(i, (i + by) % peers) for i in range(peers)])  6.95 us
    all_to_all x1, starting transfers between devices, exchange_x(): return lax.all_to_all(x, 'x', 0, 0, tiled=True)  4.01 us
    all_to_all x1, waiting for transfers between devices, exchange_x(): return lax.all_to_all(x, 'x', 0, 0, tiled=True)  3.25 us
  transfers between devices with their start and end apart: 4, of which 3 were waited for; matrix products, arithmetic and copies ran while one was open for 0% of the time, Pallas kernels for 9%

profile of v4, /device:TPU:1, one launch (start us, length us, event | category | flops | bytes accessed | tf_op | source)
XLA Modules:
  0.0 82.4 jit_solution(3755058431409280452)
XLA Ops:
  0.6 0.1 iota.11
  0.7 1.0 %bitcast_select_fusion.own = bf16[512,128]{1,0:T(8,128)(2,1)S(1)} fusion(pred[512]{0:T(512)(128)(4,1)S(1)} %iota.12, bf16[256,128]{1,0:T(8,128)(2,1)} %param.9, bf16[256,128]{1,0:T(8,128)(2,1)} %param.8), kind=kLoop, calls=%fused_computation | loop fusion | flops 65536 | bytes 262656 | tf_op jit(solution)/shard_map/jit(_where)/select_n | solution.py:252
  1.7 0.0 copy-start
  1.8 0.0 copy-start.1
  1.8 4.5 %collective-permute-start = (bf16[512,128]{1,0:T(8,128)(2,1)S(1)}, bf16[512,128]{1,0:T(8,128)(2,1)S(1)}, u32[]{:S(2)}, u32[]{:S(2)}) collective-permute-start(bf16[512,128]{1,0:T(8,128)(2,1)S(1)} %bitcast_select_fusion.own), channel_id=1, source_target_pairs={{0,32},{32,64},{64,96},{96,128},{128,160},{160,192},{192,224},{224... | collective-permute-start | bytes 393224 | tf_op jit(solution)/shard_map/ppermute | solution.py:242
  6.3 0.0 copy-start.2
  6.3 0.7 copy-done.2
  7.0 0.0 copy-start.3
  7.0 2.3 %shard_map.102.ext = bf16[256,128]{1,0:T(8,128)(2,1)S(1)} custom-call(bf16[256,2048]{1,0:T(8,128)(2,1)} %g.3, bf16[256,2048]{1,0:T(8,128)(2,1)} %o_hbm.1, f32[16,256]{1,0:T(8,128)S(1)} %copy-done.2), custom_call_target="tpu_custom_call" | custom-call | flops 1342177280 | bytes 4194304 | tf_op jit(solution)/shard_map/pallas_call | solution.py:223
  9.3 7.7 %collective-permute-done.far = bf16[512,128]{1,0:T(8,128)(2,1)S(1)} collective-permute-done((bf16[512,128]{1,0:T(8,128)(2,1)S(1)}, bf16[512,128]{1,0:T(8,128)(2,1)S(1)}, u32[]{:S(2)}, u32[]{:S(2)}) %collective-permute-start) | collective-permute-done | bytes 131104 | tf_op jit(solution)/shard_map/ppermute | solution.py:242
  17.1 0.8 %shard_map.103 = bf16[4,512,128]{2,1,0:T(8,128)(2,1)} custom-call(bf16[512,128]{1,0:T(8,128)(2,1)S(1)} %bitcast_select_fusion.own, bf16[512,128]{1,0:T(8,128)(2,1)S(1)} %collective-permute-done.far), custom_call_target="tpu_custom_call" | custom-call | bytes 4194304 | tf_op jit(solution)/shard_map/pallas_call | solution.py:223
  17.9 4.0 %all-to-all-start = ((bf16[4,512,128]{2,1,0:T(8,128)(2,1)}), bf16[4,512,128]{2,1,0:T(8,128)(2,1)S(1)}, u32[]{:S(2)}, u32[]{:S(2)}) async-start(bf16[4,512,128]{2,1,0:T(8,128)(2,1)} %shard_map.103), calls=%async_computation | async-start | bytes 1048576 | tf_op jit(solution)/shard_map/all_to_all | solution.py:237
  21.9 0.0 copy-done
  21.9 0.0 copy-done.1
  21.9 0.0 copy-done.3
  21.9 4.4 %shard_map.104 = (f32[4096,128]{1,0:T(8,128)}, f32[512,128]{1,0:T(8,128)S(1)}, bf16[512,128]{1,0:T(8,128)(2,1)S(1)}) custom-call(s32[256]{0:T(256)S(1)} %copy-done.3, s32[1,256]{1,0:T(1,128)S(1)} %bitcast.17, bf16[256,2048]{1,0:T(8,128)(2,1)S(1)} %copy-done, bf16[256,2048]{1,0:T(8,128)(2,1)S(1)} %copy-done.1, bf16[256,128]{1,0:T(8,128)(2,1)S(1)} %shard_map.102.ext, ...), custom_call_target="tpu_custom_call" | custom-call | flops 2684354560 | bytes 4194304 | tf_op jit(solution)/shard_map/pallas_call | solution.py:223
  26.4 3.2 %all-to-all-done.blocks = bf16[4,512,128]{2,1,0:T(8,128)(2,1)S(1)} async-done(((bf16[4,512,128]{2,1,0:T(8,128)(2,1)}), bf16[4,512,128]{2,1,0:T(8,128)(2,1)S(1)}, u32[]{:S(2)}, u32[]{:S(2)}) %all-to-all-start) | async-done | bytes 524320 | tf_op jit(solution)/shard_map/all_to_all | solution.py:237
  29.6 3.3 %shard_map.105 = (bf16[256,2048]{1,0:T(8,128)(2,1)}, bf16[4,528,128]{2,1,0:T(8,128)(2,1)S(1)}) custom-call(s32[256]{0:T(256)S(1)} %copy-done.3, s32[1,256]{1,0:T(1,128)S(1)} %bitcast.18, bf16[256,2048]{1,0:T(8,128)(2,1)S(1)} %copy-done, bf16[256,2048]{1,0:T(8,128)(2,1)S(1)} %copy-done.1, bf16[256,128]{1,0:T(8,128)(2,1)S(1)} %shard_map.102.ext, ...), custom_call_target="tpu_custom_call" | custom-call | flops 4026531840 | bytes 4194304 | tf_op jit(solution)/shard_map/pallas_call | solution.py:223
  33.0 15.1 %all_to_all.32.back = bf16[4,528,128]{2,1,0:T(8,128)(2,1)S(1)} all-to-all(bf16[4,528,128]{2,1,0:T(8,128)(2,1)S(1)} %get-tuple-element.29), channel_id=1, replica_groups=mesh['z'=16,'x'=4,'y'=4,'core'=2] {'x'}, dimensions={0} | all-to-all | bytes 1081344 | tf_op jit(solution)/shard_map/all_to_all | solution.py:237
  48.0 0.6 shard_map.106.rows
  48.7 8.6 %all-to-all-start.2 = ((f32[8,1,128]{2,1,0:T(1,128)}), f32[8,1,128]{2,1,0:T(1,128)S(1)}, u32[]{:S(2)}, u32[]{:S(2)}) async-start(f32[8,1,128]{2,1,0:T(1,128)} %bitcast.4), calls=%async_computation.2 | async-start | bytes 8192 | tf_op jit(solution)/shard_map/all_to_all | solution.py:289
  57.3 0.9 %shard_map.108 = (f32[512,128]{1,0:T(8,128)S(1)}, bf16[512,128]{1,0:T(8,128)(2,1)S(1)}) custom-call(bf16[4,528,128]{2,1,0:T(8,128)(2,1)S(1)} %all_to_all.32.back, f32[512,128]{1,0:T(8,128)S(1)} %get-tuple-element.30.own_grads, f32[8,128]{1,0:T(8,128)} %shard_map.106.rows), custom_call_target="tpu_custom_call" | custom-call | flops 6710886400 | bytes 4194304 | tf_op jit(solution)/shard_map/pallas_call | solution.py:223
  58.2 2.4 %collective-permute-start.1 = (bf16[512,128]{1,0:T(8,128)(2,1)S(1)}, bf16[512,128]{1,0:T(8,128)(2,1)S(1)}, u32[]{:S(2)}, u32[]{:S(2)}) collective-permute-start(bf16[512,128]{1,0:T(8,128)(2,1)S(1)} %get-tuple-element.32), channel_id=1, source_target_pairs={{0,480},{32,0},{64,32},{96,64},{128,96},{160,128},{192,160},{224,1... | collective-permute-start | bytes 393224 | tf_op jit(solution)/shard_map/ppermute | solution.py:242
  60.7 1.1 %all-to-all-done.2 = f32[8,1,128]{2,1,0:T(1,128)S(1)} async-done(((f32[8,1,128]{2,1,0:T(1,128)}), f32[8,1,128]{2,1,0:T(1,128)S(1)}, u32[]{:S(2)}, u32[]{:S(2)}) %all-to-all-start.2) | async-done | bytes 4128 | tf_op jit(solution)/shard_map/all_to_all | solution.py:289
  61.8 19.9 %all_to_all.33 = f32[16,1,128]{2,1,0:T(1,128)S(1)} all-to-all(f32[16,1,128]{2,1,0:T(1,128)S(1)} %bitcast.15), channel_id=1, replica_groups=mesh['z'=16,'x'=4,'y'=4,'core'=2] {'z'}, dimensions={0} | all-to-all | bytes 16384 | tf_op jit(solution)/shard_map/all_to_all | solution.py:295
  81.7 0.0 collective-permute-done.1.arrived
  81.7 0.7 shard_map.109
  (3 shorter events, 0.0 us)
Async XLA Ops:
  1.7 20.2 %copy-start = (bf16[256,2048]{1,0:T(8,128)(2,1)S(1)}, bf16[256,2048]{1,0:T(8,128)(2,1)}, u32[]{:S(2)}) copy-start(bf16[256,2048]{1,0:T(8,128)(2,1)} %q.3) | copy-start | bytes 3145732
  1.8 20.2 %copy-start.1 = (bf16[256,2048]{1,0:T(8,128)(2,1)S(1)}, bf16[256,2048]{1,0:T(8,128)(2,1)}, u32[]{:S(2)}) copy-start(bf16[256,2048]{1,0:T(8,128)(2,1)} %g.3) | copy-start | bytes 3145732
  1.8 15.3 %collective-permute-start = (bf16[512,128]{1,0:T(8,128)(2,1)S(1)}, bf16[512,128]{1,0:T(8,128)(2,1)S(1)}, u32[]{:S(2)}, u32[]{:S(2)}) collective-permute-start(bf16[512,128]{1,0:T(8,128)(2,1)S(1)} %bitcast_select_fusion.own), channel_id=1, source_target_pairs={{0,32},{32,64},{64,96},{96,128},{128,160},{160,192},{192,224},{224... | collective-permute-start | bytes 393224 | tf_op jit(solution)/shard_map/ppermute | solution.py:242
  6.3 0.7 copy-start.2
  7.0 14.9 %copy-start.3 = (s32[256]{0:T(256)S(1)}, s32[256]{0:T(256)}, u32[]{:S(2)}) copy-start(s32[256]{0:T(256)} %first.3) | copy-start | bytes 3076
  17.9 11.7 %all-to-all-start = ((bf16[4,512,128]{2,1,0:T(8,128)(2,1)}), bf16[4,512,128]{2,1,0:T(8,128)(2,1)S(1)}, u32[]{:S(2)}, u32[]{:S(2)}) async-start(bf16[4,512,128]{2,1,0:T(8,128)(2,1)} %shard_map.103), calls=%async_computation | async-start | bytes 1048576 | tf_op jit(solution)/shard_map/all_to_all | solution.py:237
  48.7 13.1 %all-to-all-start.2 = ((f32[8,1,128]{2,1,0:T(1,128)}), f32[8,1,128]{2,1,0:T(1,128)S(1)}, u32[]{:S(2)}, u32[]{:S(2)}) async-start(f32[8,1,128]{2,1,0:T(1,128)} %bitcast.4), calls=%async_computation.2 | async-start | bytes 8192 | tf_op jit(solution)/shard_map/all_to_all | solution.py:289
  58.2 23.5 %collective-permute-start.1 = (bf16[512,128]{1,0:T(8,128)(2,1)S(1)}, bf16[512,128]{1,0:T(8,128)(2,1)S(1)}, u32[]{:S(2)}, u32[]{:S(2)}) collective-permute-start(bf16[512,128]{1,0:T(8,128)(2,1)S(1)} %get-tuple-element.32), channel_id=1, source_target_pairs={{0,480},{32,0},{64,32},{96,64},{128,96},{160,128},{192,160},{224,1... | collective-permute-start | bytes 393224 | tf_op jit(solution)/shard_map/ppermute | solution.py:242

commit v5 on v3

--- a/solution.py
+++ b/solution.py
@@ -98,7 +98,7 @@
     ext[...] = ext_t[...].T.astype(BF16)
 
 
-def tile_grads(q, g, ext, k, v, bias, dq, dkv):
+def tile_grads(q, g, ext, k, v, bias, dq, dkv, finish=None):
     lane = lax.broadcasted_iota(jnp.int32, (ROWS, HD), 1)
     k_wide = jnp.concatenate([k, jnp.where(lane % 8 < 3, 1.0, 0.0).astype(BF16)], axis=1)
     v_wide = jnp.concatenate([v, jnp.where((lane % 8 >= 3) & (lane % 8 < 6), 1.0, 0.0).astype(BF16)], axis=1)
@@ -110,6 +110,8 @@
     probs = jnp.exp2(scores * (SCALE * LOG2E) + jnp.concatenate([bias[...]] * HEADS, axis=0))
     dscores = (probs * dprobs).astype(BF16)
     dq[...] += dot(dscores, k)
+    if finish is not None:
+        finish()
     q_rows = jnp.concatenate([q[:, columns(h)] for h in range(HEADS)], axis=0)
     g_rows = jnp.concatenate([g[:, columns(h)] for h in range(HEADS)], axis=0)
     dkv[:, :ROWS] = dot(q_rows, dscores, TN) * SCALE
@@ -155,34 +157,46 @@
     parts[x, : 2 * ROWS] = far_grads[...]
     reach = jnp.clip(lax.div(ctx * ROWS - first[0] + (ROWS - 1), ROWS), 0, REACH - 1)
 
-    def one(offset, carry):
+    copies = chunk_copies(dq, dq_hbm, dq_sems)
+
+    def finish():
+        square = jnp.zeros((8, HD), F32)
+        for h in range(HEADS):
+            block = (total[rows_of(h), :] + near[rows_of(h), :]) * SCALE
+            dq[:, columns(h)] = block.astype(BF16)
+            square += jnp.sum((block * block).reshape(ROWS // 8, 8, HD), axis=0)
+            if (h + 1) % (HEADS // CHUNKS) == 0:
+                copies[h // (HEADS // CHUNKS)].start()
+        square = jnp.broadcast_to(jnp.sum(square, axis=0, keepdims=True), (TAIL, HD))
+        place = lax.broadcasted_iota(jnp.int32, (TAIL, HD), 0)
+        rows = jnp.zeros((TAIL, HD), F32)
+        for r, term in enumerate(pieces(square)):
+            rows = jnp.where(place == r, term, rows)
+        for i in range(ROW_X):
+            parts[i, 2 * ROWS :] = rows.astype(BF16)
+
+    def one(offset, finish):
         slot = lax.rem(x - offset + ROW_X, ROW_X)
         set_bias(bias, doc, ctx, offset)
-        tile_grads(q, g, ext, blocks[slot, :ROWS], blocks[slot, ROWS:], bias, total, dkv)
+        tile_grads(q, g, ext, blocks[slot, :ROWS], blocks[slot, ROWS:], bias, total, dkv, finish)
         parts[slot, :ROWS] = dkv[:, :ROWS].T.astype(BF16)
         parts[slot, ROWS : 2 * ROWS] = dkv[:, ROWS:].T.astype(BF16)
+
+    def nearer(offset, carry):
+        one(offset, None)
         return carry
 
-    lax.fori_loop(1, reach + 1, one, 0)
+    lax.fori_loop(1, reach, nearer, 0)
     near_copy.wait()
-    copies = chunk_copies(dq, dq_hbm, dq_sems)
-    for h in range(HEADS):
-        block = (total[rows_of(h), :] + near[rows_of(h), :]) * SCALE
-        total[rows_of(h), :] = block
-        dq[:, columns(h)] = block.astype(BF16)
-        if (h + 1) % (HEADS // CHUNKS) == 0:
-            copies[h // (HEADS // CHUNKS)].start()
-    square = jnp.zeros((8, HD), F32)
-    for h in range(HEADS):
-        block = total[rows_of(h), :]
-        square += jnp.sum((block * block).reshape(ROWS // 8, 8, HD), axis=0)
-    square = jnp.broadcast_to(jnp.sum(square, axis=0, keepdims=True), (TAIL, HD))
-    place = lax.broadcasted_iota(jnp.int32, (TAIL, HD), 0)
-    rows = jnp.zeros((TAIL, HD), F32)
-    for r, term in enumerate(pieces(square)):
-        rows = jnp.where(place == r, term, rows)
-    for i in range(ROW_X):
-        parts[i, 2 * ROWS :] = rows.astype(BF16)
+
+    @pl.when(reach > 0)
+    def _():
+        one(reach, finish)
+
+    @pl.when(reach == 0)
+    def _():
+        finish()
+
     wait_all(copies)
 
 

time: 78.7 us -> 80.2 us (1.019)
  starting transfers between devices: 27.7 us -> 29.2 us
    all_to_all x1, starting transfers between devices: 14 us -> 15.5 us  [shards(): squares = lax.all_to_all(rows, members, 0, 0, tiled=True)]
where the time goes in v5:
time: 80.2 us; the launch traced here: 79.3 us
  starting transfers between devices  29.2 us (36%)
  waiting for transfers between devices  20.6 us (26%)
  blocking collectives  14.7 us (18%)
  Pallas kernels  12.3 us (15%)
  other arithmetic  1.01 us (1%)
  local copies, waits for them, and re-layouts  0.82 us (1%)
    all_to_all x1, starting transfers between devices, shards(): squares = lax.all_to_all(rows, members, 0, 0, tiled=True)  15.5 us
    all_to_all x1, blocking collectives, exchange_x(): return lax.all_to_all(x, 'x', 0, 0, tiled=True)  14.7 us
    pallas_call x6, Pallas kernels, call(): pl.pallas_call(kernel, out_shape=tuple((jax.ShapeDtypeStruct(shape, dtype...  12.3 us
    ppermute x2, waiting for transfers between devices, shift_z(): return lax.ppermute(x, 'z', [(i, (i + by) % peers) for i in range(peers)])  10.8 us
    ppermute x2, starting transfers between devices, shift_z(): return lax.ppermute(x, 'z', [(i, (i + by) % peers) for i in range(peers)])  9.71 us
    all_to_all x1, waiting for transfers between devices, shards(): squares = lax.all_to_all(rows, members, 0, 0, tiled=True)  6.55 us
    all_to_all x1, starting transfers between devices, exchange_x(): return lax.all_to_all(x, 'x', 0, 0, tiled=True)  4.01 us
    all_to_all x1, waiting for transfers between devices, exchange_x(): return lax.all_to_all(x, 'x', 0, 0, tiled=True)  3.25 us
  transfers between devices with their start and end apart: 4, of which 4 were waited for; matrix products, arithmetic and copies ran while one was open for 0% of the time, Pallas kernels for 9%

profile of v5, /device:TPU:1, one launch (start us, length us, event | category | flops | bytes accessed | tf_op | source)
XLA Modules:
  0.0 79.3 jit_solution(4602264573362683241)
XLA Ops:
  0.6 0.1 iota.11
  0.7 1.0 %bitcast_select_fusion.own = bf16[512,128]{1,0:T(8,128)(2,1)S(1)} fusion(pred[512]{0:T(512)(128)(4,1)S(1)} %iota.12, bf16[256,128]{1,0:T(8,128)(2,1)} %param.9, bf16[256,128]{1,0:T(8,128)(2,1)} %param.8), kind=kLoop, calls=%fused_computation | loop fusion | flops 65536 | bytes 262656 | tf_op jit(solution)/shard_map/jit(_where)/select_n | solution.py:259
  1.7 0.0 copy-start
  1.8 0.0 copy-start.1
  1.8 4.5 %collective-permute-start = (bf16[512,128]{1,0:T(8,128)(2,1)S(1)}, bf16[512,128]{1,0:T(8,128)(2,1)S(1)}, u32[]{:S(2)}, u32[]{:S(2)}) collective-permute-start(bf16[512,128]{1,0:T(8,128)(2,1)S(1)} %bitcast_select_fusion.own), channel_id=1, source_target_pairs={{0,32},{32,64},{64,96},{96,128},{128,160},{160,192},{192,224},{224... | collective-permute-start | bytes 393224 | tf_op jit(solution)/shard_map/ppermute | solution.py:249
  6.3 0.0 copy-start.2
  6.3 0.7 copy-done.2
  7.0 0.0 copy-start.3
  7.0 2.3 %shard_map.102.ext = bf16[256,128]{1,0:T(8,128)(2,1)S(1)} custom-call(bf16[256,2048]{1,0:T(8,128)(2,1)} %g.3, bf16[256,2048]{1,0:T(8,128)(2,1)} %o_hbm.1, f32[16,256]{1,0:T(8,128)S(1)} %copy-done.2), custom_call_target="tpu_custom_call" | custom-call | flops 1342177280 | bytes 4194304 | tf_op jit(solution)/shard_map/pallas_call | solution.py:230
  9.3 7.7 %collective-permute-done.far = bf16[512,128]{1,0:T(8,128)(2,1)S(1)} collective-permute-done((bf16[512,128]{1,0:T(8,128)(2,1)S(1)}, bf16[512,128]{1,0:T(8,128)(2,1)S(1)}, u32[]{:S(2)}, u32[]{:S(2)}) %collective-permute-start) | collective-permute-done | bytes 131104 | tf_op jit(solution)/shard_map/ppermute | solution.py:249
  17.1 0.8 %shard_map.103 = bf16[4,512,128]{2,1,0:T(8,128)(2,1)} custom-call(bf16[512,128]{1,0:T(8,128)(2,1)S(1)} %bitcast_select_fusion.own, bf16[512,128]{1,0:T(8,128)(2,1)S(1)} %collective-permute-done.far), custom_call_target="tpu_custom_call" | custom-call | bytes 4194304 | tf_op jit(solution)/shard_map/pallas_call | solution.py:230
  17.9 4.0 %all-to-all-start = ((bf16[4,512,128]{2,1,0:T(8,128)(2,1)}), bf16[4,512,128]{2,1,0:T(8,128)(2,1)S(1)}, u32[]{:S(2)}, u32[]{:S(2)}) async-start(bf16[4,512,128]{2,1,0:T(8,128)(2,1)} %shard_map.103), calls=%async_computation | async-start | bytes 1048576 | tf_op jit(solution)/shard_map/all_to_all | solution.py:244
  21.9 0.0 copy-done
  21.9 0.0 copy-done.1
  21.9 0.0 copy-done.3
  21.9 4.4 %shard_map.104 = (f32[4096,128]{1,0:T(8,128)}, f32[512,128]{1,0:T(8,128)S(1)}, bf16[512,128]{1,0:T(8,128)(2,1)S(1)}) custom-call(s32[256]{0:T(256)S(1)} %copy-done.3, s32[1,256]{1,0:T(1,128)S(1)} %bitcast.11, bf16[256,2048]{1,0:T(8,128)(2,1)S(1)} %copy-done, bf16[256,2048]{1,0:T(8,128)(2,1)S(1)} %copy-done.1, bf16[256,128]{1,0:T(8,128)(2,1)S(1)} %shard_map.102.ext, ...), custom_call_target="tpu_custom_call" | custom-call | flops 2684354560 | bytes 4194304 | tf_op jit(solution)/shard_map/pallas_call | solution.py:230
  26.4 3.2 %all-to-all-done.blocks = bf16[4,512,128]{2,1,0:T(8,128)(2,1)S(1)} async-done(((bf16[4,512,128]{2,1,0:T(8,128)(2,1)}), bf16[4,512,128]{2,1,0:T(8,128)(2,1)S(1)}, u32[]{:S(2)}, u32[]{:S(2)}) %all-to-all-start) | async-done | bytes 524320 | tf_op jit(solution)/shard_map/all_to_all | solution.py:244
  29.6 3.2 %shard_map.105 = (bf16[256,2048]{1,0:T(8,128)(2,1)}, bf16[4,528,128]{2,1,0:T(8,128)(2,1)S(1)}) custom-call(s32[256]{0:T(256)S(1)} %copy-done.3, s32[1,256]{1,0:T(1,128)S(1)} %bitcast.12, bf16[256,2048]{1,0:T(8,128)(2,1)S(1)} %copy-done, bf16[256,2048]{1,0:T(8,128)(2,1)S(1)} %copy-done.1, bf16[256,128]{1,0:T(8,128)(2,1)S(1)} %shard_map.102.ext, ...), custom_call_target="tpu_custom_call" | custom-call | flops 4026531840 | bytes 4194304 | tf_op jit(solution)/shard_map/pallas_call | solution.py:230
  32.9 14.7 %all_to_all.21.back = bf16[4,528,128]{2,1,0:T(8,128)(2,1)S(1)} all-to-all(bf16[4,528,128]{2,1,0:T(8,128)(2,1)S(1)} %get-tuple-element.30), channel_id=1, replica_groups=mesh['z'=16,'x'=4,'y'=4,'core'=2] {'x'}, dimensions={0} | all-to-all | bytes 1081344 | tf_op jit(solution)/shard_map/all_to_all | solution.py:244
  47.6 0.7 shard_map.106
  48.3 15.5 %all-to-all-start.2 = ((f32[128,1,128]{2,1,0:T(1,128)}), f32[128,1,128]{2,1,0:T(1,128)S(1)}, u32[]{:S(2)}, u32[]{:S(2)}) async-start(f32[128,1,128]{2,1,0:T(1,128)} %bitcast.4), calls=%async_computation.2 | async-start | bytes 131072 | tf_op jit(solution)/shard_map/all_to_all | solution.py:303
  63.8 5.2 %collective-permute-start.1 = (bf16[512,128]{1,0:T(8,128)(2,1)S(1)}, bf16[512,128]{1,0:T(8,128)(2,1)S(1)}, u32[]{:S(2)}, u32[]{:S(2)}) collective-permute-start(bf16[512,128]{1,0:T(8,128)(2,1)S(1)} %get-tuple-element.34), channel_id=1, source_target_pairs={{0,480},{32,0},{64,32},{96,64},{128,96},{160,128},{192,160},{224,1... | collective-permute-start | bytes 393224 | tf_op jit(solution)/shard_map/ppermute | solution.py:249
  69.0 3.1 %collective-permute-done.1.arrived = bf16[512,128]{1,0:T(8,128)(2,1)S(1)} collective-permute-done((bf16[512,128]{1,0:T(8,128)(2,1)S(1)}, bf16[512,128]{1,0:T(8,128)(2,1)S(1)}, u32[]{:S(2)}, u32[]{:S(2)}) %collective-permute-start.1) | collective-permute-done | bytes 131104 | tf_op jit(solution)/shard_map/ppermute | solution.py:249
  72.1 6.5 %all-to-all-done.2 = f32[128,1,128]{2,1,0:T(1,128)S(1)} async-done(((f32[128,1,128]{2,1,0:T(1,128)}), f32[128,1,128]{2,1,0:T(1,128)S(1)}, u32[]{:S(2)}, u32[]{:S(2)}) %all-to-all-start.2) | async-done | bytes 65568 | tf_op jit(solution)/shard_map/all_to_all | solution.py:303
  78.6 0.7 shard_map.107
  (2 shorter events, 0.0 us)
Async XLA Ops:
  1.7 20.2 %copy-start = (bf16[256,2048]{1,0:T(8,128)(2,1)S(1)}, bf16[256,2048]{1,0:T(8,128)(2,1)}, u32[]{:S(2)}) copy-start(bf16[256,2048]{1,0:T(8,128)(2,1)} %q.3) | copy-start | bytes 3145732
  1.8 20.2 %copy-start.1 = (bf16[256,2048]{1,0:T(8,128)(2,1)S(1)}, bf16[256,2048]{1,0:T(8,128)(2,1)}, u32[]{:S(2)}) copy-start(bf16[256,2048]{1,0:T(8,128)(2,1)} %g.3) | copy-start | bytes 3145732
  1.8 15.3 %collective-permute-start = (bf16[512,128]{1,0:T(8,128)(2,1)S(1)}, bf16[512,128]{1,0:T(8,128)(2,1)S(1)}, u32[]{:S(2)}, u32[]{:S(2)}) collective-permute-start(bf16[512,128]{1,0:T(8,128)(2,1)S(1)} %bitcast_select_fusion.own), channel_id=1, source_target_pairs={{0,32},{32,64},{64,96},{96,128},{128,160},{160,192},{192,224},{224... | collective-permute-start | bytes 393224 | tf_op jit(solution)/shard_map/ppermute | solution.py:249
  6.3 0.7 copy-start.2
  7.0 14.9 %copy-start.3 = (s32[256]{0:T(256)S(1)}, s32[256]{0:T(256)}, u32[]{:S(2)}) copy-start(s32[256]{0:T(256)} %first.3) | copy-start | bytes 3076
  17.9 11.7 %all-to-all-start = ((bf16[4,512,128]{2,1,0:T(8,128)(2,1)}), bf16[4,512,128]{2,1,0:T(8,128)(2,1)S(1)}, u32[]{:S(2)}, u32[]{:S(2)}) async-start(bf16[4,512,128]{2,1,0:T(8,128)(2,1)} %shard_map.103), calls=%async_computation | async-start | bytes 1048576 | tf_op jit(solution)/shard_map/all_to_all | solution.py:244
  48.3 30.3 %all-to-all-start.2 = ((f32[128,1,128]{2,1,0:T(1,128)}), f32[128,1,128]{2,1,0:T(1,128)S(1)}, u32[]{:S(2)}, u32[]{:S(2)}) async-start(f32[128,1,128]{2,1,0:T(1,128)} %bitcast.4), calls=%async_computation.2 | async-start | bytes 131072 | tf_op jit(solution)/shard_map/all_to_all | solution.py:303
  63.8 8.3 %collective-permute-start.1 = (bf16[512,128]{1,0:T(8,128)(2,1)S(1)}, bf16[512,128]{1,0:T(8,128)(2,1)S(1)}, u32[]{:S(2)}, u32[]{:S(2)}) collective-permute-start(bf16[512,128]{1,0:T(8,128)(2,1)S(1)} %get-tuple-element.34), channel_id=1, source_target_pairs={{0,480},{32,0},{64,32},{96,64},{128,96},{160,128},{192,160},{224,1... | collective-permute-start | bytes 393224 | tf_op jit(solution)/shard_map/ppermute | solution.py:249
